TPU v7x, 512 devices: a whole 4x8x8 slice. The times are simulated.
512 devices in a mesh: space: 32 (over x, z), probe: 16 (over y, core).
Axes of the slice: x: 4, y: 8, z: 8, core: 2. Of those that a mesh axis runs over, the one named last changes fastest.
Arguments:
- conductivity: float32 [256, 8192], P('space'), may hold values from 1 to 2
- leakage: float32 [256, 8192], P('space'), may hold values from 0.005 to 0.05
- signs: int32 [64, 256], P('probe'), may hold values from 0 to 1
- wells: int32 [256], replicated, may hold values from 0 to 2097151
Outputs:
- basis: float32 [64, 2097152], P(None, ('space', 'probe'))
- factor: float32 [64, 64], replicated
Inputs may be any that keep to these rules, and one draw needn't show every extreme that they name: Probe k gives well w the sign 2 signs[k, w] - 1. Flat cell indices; wells may repeat.
All inputs are finite; a program needn't handle non-finite values.
Results may differ from a plain program's by a relative error of at most 0.0003.
Values sent between devices are 32-bit elements; how exact they have to be, the bound alone decides.
A program may use at most 128 MiB of HBM per device.

v0:
```python
import math

import jax
import jax.numpy as jnp
from jax import lax
from jax.sharding import PartitionSpec as P

NZ = 64
SWEEPS = 16


bound_low = 0.005
bound_high = 24.5


def padded_2(cells, sides, width):
    for axis, dim in sides:
        count = lax.axis_size(axis)
        ends = count - 1
        head = lax.slice_in_dim(cells, 0, width, axis=dim)
        tail = lax.slice_in_dim(cells, cells.shape[dim] - width, cells.shape[dim], axis=dim)
        cells = jnp.concatenate(
            [
                lax.ppermute(tail, axis, [(i, (i + 1) % count) for i in range(ends)]),
                cells,
                lax.ppermute(head, axis, [((i + 1) % count, i) for i in range(ends)]),
            ],
            axis=dim,
        )
    return cells


def chebyshev_table(count):
    center = 0.5 * (bound_high + bound_low)
    spread = 0.5 * (bound_high - bound_low)
    ratio = center / spread
    rho_prev = 1.0 / ratio
    entries = []
    for index_step in range(count):
        rho_next = 1.0 / (2.0 * ratio - rho_prev)
        entries.append([rho_next * rho_prev, 2.0 * rho_next / spread])
        rho_prev = rho_next
    return jnp.array(entries, dtype=jnp.float32)


def start_scale():
    return 1.0 / (0.5 * (bound_high + bound_low))


def apply_operator(extended, faces, low_z, high_z, layer):
    centre = extended[..., 1:-1, :]
    below_x = extended[..., :-2, :]
    above_x = extended[..., 2:, :]
    zeros_y = jnp.zeros(centre.shape[:-1] + (layer,), jnp.float32)
    below_y = jnp.concatenate([zeros_y, centre[..., :-layer]], -1)
    above_y = jnp.concatenate([centre[..., layer:], zeros_y], -1)
    zero_z = jnp.zeros(centre.shape[:-1] + (1,), jnp.float32)
    below_z = jnp.concatenate([zero_z, centre[..., :-1]], -1) * low_z
    above_z = jnp.concatenate([centre[..., 1:], zero_z], -1) * high_z
    result = faces[0] * centre + faces[1] * (centre - below_x)
    result = result + faces[2] * (centre - above_x)
    result = result + faces[3] * (centre - below_y)
    result = result + faces[4] * (centre - above_y)
    result = result + faces[5] * (centre - below_z)
    result = result + faces[6] * (centre - above_z)
    return result


def on_device(conductivity, leakage, signs, wells):
    rows = conductivity.shape[0]
    columns = conductivity.shape[1]
    plane_y = columns // NZ
    space_count = lax.axis_size("space")
    here = lax.axis_index("space")
    depth = 1
    props = jnp.stack([conductivity, leakage])
    widened = padded_2(props, (("space", 1),), depth)
    first_rows = jnp.where(here == 0, props[:, :1], widened[:, :depth])
    last_rows = jnp.where(here == space_count - 1, props[:, -1:], widened[:, -depth:])
    widened = jnp.concatenate([first_rows, props, last_rows], 1)
    kappa_all = widened[0]
    middle = kappa_all[1:-1]
    span = middle.shape[0]
    cube = middle.reshape(span, plane_y, NZ)
    padded = jnp.pad(cube, ((0, 0), (1, 1), (1, 1)), mode="edge")
    faces = (
        widened[1][1:-1],
        0.5 * (middle + kappa_all[:-2]),
        0.5 * (middle + kappa_all[2:]),
        (0.5 * (cube + padded[:, :-2, 1:-1])).reshape(span, columns),
        (0.5 * (cube + padded[:, 2:, 1:-1])).reshape(span, columns),
        (0.5 * (cube + padded[:, 1:-1, :-2])).reshape(span, columns),
        (0.5 * (cube + padded[:, 1:-1, 2:])).reshape(span, columns),
    )
    depth_z = jnp.arange(columns, dtype=jnp.int32) % NZ
    low_z = (depth_z != 0).astype(jnp.float32)
    high_z = (depth_z != NZ - 1).astype(jnp.float32)
    local_probes = signs.shape[0]
    start_cell = here * (rows * columns)
    offset = wells - start_cell
    inside = (offset >= 0) & (offset < rows * columns)
    position = jnp.where(inside, offset, 0)
    weights = (2 * signs - 1).astype(jnp.float32) * inside.astype(jnp.float32)[None, :]
    sources = jnp.zeros((local_probes, rows * columns), jnp.float32).at[:, position].add(weights)
    sources = sources.reshape(local_probes, rows, columns)
    table = chebyshev_table(SWEEPS)
    start = (jnp.zeros_like(sources), sources, sources * start_scale())

    def single(step, carry):
        iterate, resid, search = carry
        grown = padded_2(search, (("space", 1),), 1)
        image = apply_operator(grown, faces, low_z, high_z, NZ)
        iterate = iterate + search
        resid = resid - image
        search = table[step, 0] * search + table[step, 1] * resid
        return (iterate, resid, search)

    final = lax.fori_loop(0, SWEEPS, single, start)
    flat_fields = final[0].reshape(local_probes, rows * columns)
    panel = lax.all_to_all(flat_fields, "probe", split_axis=1, concat_axis=0, tiled=True)
    gram_part = jnp.dot(
        panel, panel.T, precision=lax.Precision.HIGHEST, preferred_element_type=jnp.float32
    )
    gram = lax.psum(gram_part, ("space", "probe"))
    lower = jnp.linalg.cholesky(gram)
    total_cells = space_count * rows * columns
    basis = jax.scipy.linalg.solve_triangular(lower, panel, lower=True) * math.sqrt(total_cells)
    factor = lower.T / math.sqrt(wells.shape[0])
    return (basis, factor)


def solution(mesh):
    placed = (P("space", None), P("space", None), P("probe", None), P())
    return jax.shard_map(
        on_device,
        mesh=mesh,
        in_specs=placed,
        out_specs=(P(None, ("space", "probe")), P()),
        check_vma=False,
    )
```

profile of v0, /device:TPU:1, one launch (start us, length us, event | category | flops | bytes accessed | tf_op | source)
XLA Modules:
  0.0 567.2 jit_solution(7938215226388339393)
XLA Ops:
  6.4 15.5 %scatter_custom_fusion = f32[4,65536]{0,1:T(8,128)} fusion(s32[256]{0:T(256)S(1)} %compare_select_fusion, f32[256,4]{1,0:T(8,128)S(1)} %copy.13, f32[]{:T(128)} %constant.106.clone.1), kind=kCustom, calls=%fused_computation.29 | custom fusion | flops 1024 | bytes 1048580 | tf_op jit(solution)/shard_map/scatter-add | solution.py:104
  21.8 18.8 %copy.15 = f32[4,8,8192]{2,1,0:T(8,128)} copy(f32[4,8,8192]{0,2,1:T(8,128)} %bitcast.40) | data formatting | bytes 2097152
  43.3 5.5 collective-permute-start.2
  57.2 333.0 %while.20 = (s32[]{:T(128)}, f32[4,8,8192]{2,1,0:T(8,128)}, f32[4,8,8192]{2,1,0:T(8,128)}, f32[4,8,8192]{2,1,0:T(8,128)}, f32[8,8192]{1,0:T(8,128)S(1)}, /*index...) while((s32[]{:T(128)}, f32[4,8,8192]{2,1,0:T(8,128)}, ...), condition=%wide.wide.region_2.3_spmd.clone.clone, body=%wide.wide.region_1.2_spmd.sunk.clone.clone.sunk | while | flops 7684099 | bytes 25771556 | solution.py:118
  60.5 5.3 collective-permute-start.1
  70.3 6.3 %multiply_add_fusion.3 = (f32[4,8,8192]{2,1,0:T(8,128)}, f32[4,8,8192]{2,1,0:T(8,128)}) fusion(f32[4,8,8192]{2,1,0:T(8,128)S(1)} %copy.34, f32[]{:T(128)} %bitcast.38, f32[]{:T(128)} %bitcast.39, f32[4,8,8192]{2,1,0:T(8,128)} %get-tuple-element.576, f32[8192]{0:T(1024)S(1)} %get-tuple-element.546, f32[4,8,8191]{2,1,0:T(8,128)S(1)} %get-tuple-element.547, ...), kind=kLoop, calls=%fused_computation.17.clone.clone.1 | loop fusion | flops 7077888 | bytes 10534664 | tf_op jit(solution)/shard_map/while/body/eval_jaxpr/add | solution.py:115
  80.0 4.6 collective-permute-start.1
  86.6 2.3 select_add_fusion.3
  90.4 6.3 %multiply_add_fusion.3 = (f32[4,8,8192]{2,1,0:T(8,128)}, f32[4,8,8192]{2,1,0:T(8,128)}) fusion(f32[4,8,8192]{2,1,0:T(8,128)S(1)} %copy.34, f32[]{:T(128)} %bitcast.38, f32[]{:T(128)} %bitcast.39, f32[4,8,8192]{2,1,0:T(8,128)} %get-tuple-element.576, f32[8192]{0:T(1024)S(1)} %get-tuple-element.546, f32[4,8,8191]{2,1,0:T(8,128)S(1)} %get-tuple-element.547, ...), kind=kLoop, calls=%fused_computation.17.clone.clone.1 | loop fusion | flops 7077888 | bytes 10534664 | tf_op jit(solution)/shard_map/while/body/eval_jaxpr/add | solution.py:115
  100.0 5.8 %collective-permute-start.1 = (f32[4,1,8192]{2,1,0:T(1,128)}, f32[4,1,8192]{2,1,0:T(1,128)}, u32[]{:S(2)}, u32[]{:S(2)}) collective-permute-start(f32[4,1,8192]{2,1,0:T(1,128)} %get-tuple-element.553), channel_id=1, source_target_pairs={{0,16},{16,32},{32,48},{48,64},{64,80},{80,96},{96,112},{112,128},... | collective-permute-start | bytes 393224 | tf_op jit(solution)/shard_map/while/body/eval_jaxpr/ppermute | solution.py:24
  107.8 2.3 select_add_fusion.3
  111.6 6.3 %multiply_add_fusion.3 = (f32[4,8,8192]{2,1,0:T(8,128)}, f32[4,8,8192]{2,1,0:T(8,128)}) fusion(f32[4,8,8192]{2,1,0:T(8,128)S(1)} %copy.34, f32[]{:T(128)} %bitcast.38, f32[]{:T(128)} %bitcast.39, f32[4,8,8192]{2,1,0:T(8,128)} %get-tuple-element.576, f32[8192]{0:T(1024)S(1)} %get-tuple-element.546, f32[4,8,8191]{2,1,0:T(8,128)S(1)} %get-tuple-element.547, ...), kind=kLoop, calls=%fused_computation.17.clone.clone.1 | loop fusion | flops 7077888 | bytes 10534664 | tf_op jit(solution)/shard_map/while/body/eval_jaxpr/add | solution.py:115
  121.2 5.2 collective-permute-start.1
  128.4 2.3 select_add_fusion.3
  132.2 6.3 %multiply_add_fusion.3 = (f32[4,8,8192]{2,1,0:T(8,128)}, f32[4,8,8192]{2,1,0:T(8,128)}) fusion(f32[4,8,8192]{2,1,0:T(8,128)S(1)} %copy.34, f32[]{:T(128)} %bitcast.38, f32[]{:T(128)} %bitcast.39, f32[4,8,8192]{2,1,0:T(8,128)} %get-tuple-element.576, f32[8192]{0:T(1024)S(1)} %get-tuple-element.546, f32[4,8,8191]{2,1,0:T(8,128)S(1)} %get-tuple-element.547, ...), kind=kLoop, calls=%fused_computation.17.clone.clone.1 | loop fusion | flops 7077888 | bytes 10534664 | tf_op jit(solution)/shard_map/while/body/eval_jaxpr/add | solution.py:115
  141.8 5.2 collective-permute-start.1
  149.0 2.3 select_add_fusion.3
  152.8 6.3 %multiply_add_fusion.3 = (f32[4,8,8192]{2,1,0:T(8,128)}, f32[4,8,8192]{2,1,0:T(8,128)}) fusion(f32[4,8,8192]{2,1,0:T(8,128)S(1)} %copy.34, f32[]{:T(128)} %bitcast.38, f32[]{:T(128)} %bitcast.39, f32[4,8,8192]{2,1,0:T(8,128)} %get-tuple-element.576, f32[8192]{0:T(1024)S(1)} %get-tuple-element.546, f32[4,8,8191]{2,1,0:T(8,128)S(1)} %get-tuple-element.547, ...), kind=kLoop, calls=%fused_computation.17.clone.clone.1 | loop fusion | flops 7077888 | bytes 10534664 | tf_op jit(solution)/shard_map/while/body/eval_jaxpr/add | solution.py:115
  162.4 5.2 collective-permute-start.1
  169.6 2.3 select_add_fusion.3
  173.4 6.3 %multiply_add_fusion.3 = (f32[4,8,8192]{2,1,0:T(8,128)}, f32[4,8,8192]{2,1,0:T(8,128)}) fusion(f32[4,8,8192]{2,1,0:T(8,128)S(1)} %copy.34, f32[]{:T(128)} %bitcast.38, f32[]{:T(128)} %bitcast.39, f32[4,8,8192]{2,1,0:T(8,128)} %get-tuple-element.576, f32[8192]{0:T(1024)S(1)} %get-tuple-element.546, f32[4,8,8191]{2,1,0:T(8,128)S(1)} %get-tuple-element.547, ...), kind=kLoop, calls=%fused_computation.17.clone.clone.1 | loop fusion | flops 7077888 | bytes 10534664 | tf_op jit(solution)/shard_map/while/body/eval_jaxpr/add | solution.py:115
  183.0 5.2 collective-permute-start.1
  190.2 2.3 select_add_fusion.3
  194.0 6.3 %multiply_add_fusion.3 = (f32[4,8,8192]{2,1,0:T(8,128)}, f32[4,8,8192]{2,1,0:T(8,128)}) fusion(f32[4,8,8192]{2,1,0:T(8,128)S(1)} %copy.34, f32[]{:T(128)} %bitcast.38, f32[]{:T(128)} %bitcast.39, f32[4,8,8192]{2,1,0:T(8,128)} %get-tuple-element.576, f32[8192]{0:T(1024)S(1)} %get-tuple-element.546, f32[4,8,8191]{2,1,0:T(8,128)S(1)} %get-tuple-element.547, ...), kind=kLoop, calls=%fused_computation.17.clone.clone.1 | loop fusion | flops 7077888 | bytes 10534664 | tf_op jit(solution)/shard_map/while/body/eval_jaxpr/add | solution.py:115
  203.6 5.2 collective-permute-start.1
  210.8 2.3 select_add_fusion.3
  214.6 6.3 %multiply_add_fusion.3 = (f32[4,8,8192]{2,1,0:T(8,128)}, f32[4,8,8192]{2,1,0:T(8,128)}) fusion(f32[4,8,8192]{2,1,0:T(8,128)S(1)} %copy.34, f32[]{:T(128)} %bitcast.38, f32[]{:T(128)} %bitcast.39, f32[4,8,8192]{2,1,0:T(8,128)} %get-tuple-element.576, f32[8192]{0:T(1024)S(1)} %get-tuple-element.546, f32[4,8,8191]{2,1,0:T(8,128)S(1)} %get-tuple-element.547, ...), kind=kLoop, calls=%fused_computation.17.clone.clone.1 | loop fusion | flops 7077888 | bytes 10534664 | tf_op jit(solution)/shard_map/while/body/eval_jaxpr/add | solution.py:115
  224.2 5.2 collective-permute-start.1
  231.4 2.3 select_add_fusion.3
  235.2 6.3 %multiply_add_fusion.3 = (f32[4,8,8192]{2,1,0:T(8,128)}, f32[4,8,8192]{2,1,0:T(8,128)}) fusion(f32[4,8,8192]{2,1,0:T(8,128)S(1)} %copy.34, f32[]{:T(128)} %bitcast.38, f32[]{:T(128)} %bitcast.39, f32[4,8,8192]{2,1,0:T(8,128)} %get-tuple-element.576, f32[8192]{0:T(1024)S(1)} %get-tuple-element.546, f32[4,8,8191]{2,1,0:T(8,128)S(1)} %get-tuple-element.547, ...), kind=kLoop, calls=%fused_computation.17.clone.clone.1 | loop fusion | flops 7077888 | bytes 10534664 | tf_op jit(solution)/shard_map/while/body/eval_jaxpr/add | solution.py:115
  244.8 5.2 collective-permute-start.1
  255.8 6.3 %multiply_add_fusion.3 = (f32[4,8,8192]{2,1,0:T(8,128)}, f32[4,8,8192]{2,1,0:T(8,128)}) fusion(f32[4,8,8192]{2,1,0:T(8,128)S(1)} %copy.34, f32[]{:T(128)} %bitcast.38, f32[]{:T(128)} %bitcast.39, f32[4,8,8192]{2,1,0:T(8,128)} %get-tuple-element.576, f32[8192]{0:T(1024)S(1)} %get-tuple-element.546, f32[4,8,8191]{2,1,0:T(8,128)S(1)} %get-tuple-element.547, ...), kind=kLoop, calls=%fused_computation.17.clone.clone.1 | loop fusion | flops 7077888 | bytes 10534664 | tf_op jit(solution)/shard_map/while/body/eval_jaxpr/add | solution.py:115
  265.4 5.3 collective-permute-start.1
  276.5 6.3 %multiply_add_fusion.3 = (f32[4,8,8192]{2,1,0:T(8,128)}, f32[4,8,8192]{2,1,0:T(8,128)}) fusion(f32[4,8,8192]{2,1,0:T(8,128)S(1)} %copy.34, f32[]{:T(128)} %bitcast.38, f32[]{:T(128)} %bitcast.39, f32[4,8,8192]{2,1,0:T(8,128)} %get-tuple-element.576, f32[8192]{0:T(1024)S(1)} %get-tuple-element.546, f32[4,8,8191]{2,1,0:T(8,128)S(1)} %get-tuple-element.547, ...), kind=kLoop, calls=%fused_computation.17.clone.clone.1 | loop fusion | flops 7077888 | bytes 10534664 | tf_op jit(solution)/shard_map/while/body/eval_jaxpr/add | solution.py:115
  286.1 6.1 %collective-permute-start.1 = (f32[4,1,8192]{2,1,0:T(1,128)}, f32[4,1,8192]{2,1,0:T(1,128)}, u32[]{:S(2)}, u32[]{:S(2)}) collective-permute-start(f32[4,1,8192]{2,1,0:T(1,128)} %get-tuple-element.553), channel_id=1, source_target_pairs={{0,16},{16,32},{32,48},{48,64},{64,80},{80,96},{96,112},{112,128},... | collective-permute-start | bytes 393224 | tf_op jit(solution)/shard_map/while/body/eval_jaxpr/ppermute | solution.py:24
  297.9 6.3 %multiply_add_fusion.3 = (f32[4,8,8192]{2,1,0:T(8,128)}, f32[4,8,8192]{2,1,0:T(8,128)}) fusion(f32[4,8,8192]{2,1,0:T(8,128)S(1)} %copy.34, f32[]{:T(128)} %bitcast.38, f32[]{:T(128)} %bitcast.39, f32[4,8,8192]{2,1,0:T(8,128)} %get-tuple-element.576, f32[8192]{0:T(1024)S(1)} %get-tuple-element.546, f32[4,8,8191]{2,1,0:T(8,128)S(1)} %get-tuple-element.547, ...), kind=kLoop, calls=%fused_computation.17.clone.clone.1 | loop fusion | flops 7077888 | bytes 10534664 | tf_op jit(solution)/shard_map/while/body/eval_jaxpr/add | solution.py:115
  307.6 6.1 %collective-permute-start.1 = (f32[4,1,8192]{2,1,0:T(1,128)}, f32[4,1,8192]{2,1,0:T(1,128)}, u32[]{:S(2)}, u32[]{:S(2)}) collective-permute-start(f32[4,1,8192]{2,1,0:T(1,128)} %get-tuple-element.553), channel_id=1, source_target_pairs={{0,16},{16,32},{32,48},{48,64},{64,80},{80,96},{96,112},{112,128},... | collective-permute-start | bytes 393224 | tf_op jit(solution)/shard_map/while/body/eval_jaxpr/ppermute | solution.py:24
  319.4 6.3 %multiply_add_fusion.3 = (f32[4,8,8192]{2,1,0:T(8,128)}, f32[4,8,8192]{2,1,0:T(8,128)}) fusion(f32[4,8,8192]{2,1,0:T(8,128)S(1)} %copy.34, f32[]{:T(128)} %bitcast.38, f32[]{:T(128)} %bitcast.39, f32[4,8,8192]{2,1,0:T(8,128)} %get-tuple-element.576, f32[8192]{0:T(1024)S(1)} %get-tuple-element.546, f32[4,8,8191]{2,1,0:T(8,128)S(1)} %get-tuple-element.547, ...), kind=kLoop, calls=%fused_computation.17.clone.clone.1 | loop fusion | flops 7077888 | bytes 10534664 | tf_op jit(solution)/shard_map/while/body/eval_jaxpr/add | solution.py:115
  329.1 6.1 %collective-permute-start.1 = (f32[4,1,8192]{2,1,0:T(1,128)}, f32[4,1,8192]{2,1,0:T(1,128)}, u32[]{:S(2)}, u32[]{:S(2)}) collective-permute-start(f32[4,1,8192]{2,1,0:T(1,128)} %get-tuple-element.553), channel_id=1, source_target_pairs={{0,16},{16,32},{32,48},{48,64},{64,80},{80,96},{96,112},{112,128},... | collective-permute-start | bytes 393224 | tf_op jit(solution)/shard_map/while/body/eval_jaxpr/ppermute | solution.py:24
  340.9 6.3 %multiply_add_fusion.3 = (f32[4,8,8192]{2,1,0:T(8,128)}, f32[4,8,8192]{2,1,0:T(8,128)}) fusion(f32[4,8,8192]{2,1,0:T(8,128)S(1)} %copy.34, f32[]{:T(128)} %bitcast.38, f32[]{:T(128)} %bitcast.39, f32[4,8,8192]{2,1,0:T(8,128)} %get-tuple-element.576, f32[8192]{0:T(1024)S(1)} %get-tuple-element.546, f32[4,8,8191]{2,1,0:T(8,128)S(1)} %get-tuple-element.547, ...), kind=kLoop, calls=%fused_computation.17.clone.clone.1 | loop fusion | flops 7077888 | bytes 10534664 | tf_op jit(solution)/shard_map/while/body/eval_jaxpr/add | solution.py:115
  350.6 6.1 %collective-permute-start.1 = (f32[4,1,8192]{2,1,0:T(1,128)}, f32[4,1,8192]{2,1,0:T(1,128)}, u32[]{:S(2)}, u32[]{:S(2)}) collective-permute-start(f32[4,1,8192]{2,1,0:T(1,128)} %get-tuple-element.553), channel_id=1, source_target_pairs={{0,16},{16,32},{32,48},{48,64},{64,80},{80,96},{96,112},{112,128},... | collective-permute-start | bytes 393224 | tf_op jit(solution)/shard_map/while/body/eval_jaxpr/ppermute | solution.py:24
  362.4 6.3 %multiply_add_fusion.3 = (f32[4,8,8192]{2,1,0:T(8,128)}, f32[4,8,8192]{2,1,0:T(8,128)}) fusion(f32[4,8,8192]{2,1,0:T(8,128)S(1)} %copy.34, f32[]{:T(128)} %bitcast.38, f32[]{:T(128)} %bitcast.39, f32[4,8,8192]{2,1,0:T(8,128)} %get-tuple-element.576, f32[8192]{0:T(1024)S(1)} %get-tuple-element.546, f32[4,8,8191]{2,1,0:T(8,128)S(1)} %get-tuple-element.547, ...), kind=kLoop, calls=%fused_computation.17.clone.clone.1 | loop fusion | flops 7077888 | bytes 10534664 | tf_op jit(solution)/shard_map/while/body/eval_jaxpr/add | solution.py:115
  372.1 6.1 %collective-permute-start.1 = (f32[4,1,8192]{2,1,0:T(1,128)}, f32[4,1,8192]{2,1,0:T(1,128)}, u32[]{:S(2)}, u32[]{:S(2)}) collective-permute-start(f32[4,1,8192]{2,1,0:T(1,128)} %get-tuple-element.553), channel_id=1, source_target_pairs={{0,16},{16,32},{32,48},{48,64},{64,80},{80,96},{96,112},{112,128},... | collective-permute-start | bytes 393224 | tf_op jit(solution)/shard_map/while/body/eval_jaxpr/ppermute | solution.py:24
  383.9 6.3 %multiply_add_fusion.3 = (f32[4,8,8192]{2,1,0:T(8,128)}, f32[4,8,8192]{2,1,0:T(8,128)}) fusion(f32[4,8,8192]{2,1,0:T(8,128)S(1)} %copy.34, f32[]{:T(128)} %bitcast.38, f32[]{:T(128)} %bitcast.39, f32[4,8,8192]{2,1,0:T(8,128)} %get-tuple-element.576, f32[8192]{0:T(1024)S(1)} %get-tuple-element.546, f32[4,8,8191]{2,1,0:T(8,128)S(1)} %get-tuple-element.547, ...), kind=kLoop, calls=%fused_computation.17.clone.clone.1 | loop fusion | flops 7077888 | bytes 10534664 | tf_op jit(solution)/shard_map/while/body/eval_jaxpr/add | solution.py:115
  392.3 43.9 %all_to_all.19 = f32[4,16,4096]{2,0,1:T(4,128)S(1)} all-to-all(f32[4,16,4096]{2,0,1:T(4,128)S(1)} %copy.16), channel_id=1, replica_groups=mesh['space'=32,'probe'=16] {'probe'}, dimensions={1} | all-to-all | bytes 2097152 | tf_op jit(solution)/shard_map/all_to_all | solution.py:120
  437.5 114.7 %psum.7 = f32[64,64]{0,1:T(8,128)S(1)} all-reduce(f32[64,64]{0,1:T(8,128)S(1)} %fusion.47), channel_id=1, replica_groups=mesh['space'=32,'probe'=16] {'space','probe'}, use_global_device_ids=true, to_apply=%region_3.4 | all-reduce | flops 4096 | bytes 32768 | tf_op jit(solution)/shard_map/psum | solution.py:124
  552.3 5.8 %cholesky.16 = f32[64,64]{1,0:T(8,128)S(1)} custom-call(f32[64,64]{1,0:T(8,128)S(1)} %fusion.39), custom_call_target="Cholesky" | custom-call | tf_op jit(solution)/shard_map/jit(cholesky)/cholesky | solution.py:125
  559.5 4.9 custom-call.7
  (193 shorter events, 150.0 us)
Async XLA Ops:
  1.7 41.5 %collective-permute-start.3 = (f32[2,1,8192]{2,1,0:T(1,128)S(1)}, f32[2,1,8192]{2,1,0:T(1,128)S(1)}, u32[]{:S(2)}, u32[]{:S(2)}) collective-permute-start(f32[2,1,8192]{2,1,0:T(1,128)S(1)} %pad_maximum_fusion.16), channel_id=1, source_target_pairs={{16,0},{32,16},{48,32},{64,48},{80,64},{96,80},{112,96},{128,112},... | collective-permute-start | bytes 196616 | tf_op jit(solution)/shard_map/ppermute | solution.py:26
  6.4 36.8 %copy-start = (f32[8,8192]{1,0:T(8,128)S(1)}, f32[8,8192]{1,0:T(8,128)}, u32[]{:S(2)}) copy-start(f32[8,8192]{1,0:T(8,128)} %param.8) | copy-start | bytes 786436
  6.4 36.8 %copy-start.1 = (f32[8,8192]{1,0:T(8,128)S(1)}, f32[8,8192]{1,0:T(8,128)}, u32[]{:S(2)}) copy-start(f32[8,8192]{1,0:T(8,128)} %param.7) | copy-start | bytes 786436
  43.3 12.8 %collective-permute-start.2 = (f32[2,1,8192]{2,1,0:T(1,128)S(1)}, f32[2,1,8192]{2,1,0:T(1,128)S(1)}, u32[]{:S(2)}, u32[]{:S(2)}) collective-permute-start(f32[2,1,8192]{2,1,0:T(1,128)S(1)} %get-tuple-element.365), channel_id=1, source_target_pairs={{0,16},{16,32},{32,48},{48,64},{64,80},{80,96},{96,112},{112,128},... | collective-permute-start | bytes 196616 | tf_op jit(solution)/shard_map/ppermute | solution.py:24
  50.3 6.8 %copy-start.2 = (f32[8,128,64]{2,1,0:T(8,128)}, f32[8,128,64]{2,1,0:T(8,128)S(1)}, u32[]{:S(2)}) copy-start(f32[8,128,64]{2,1,0:T(8,128)S(1)} %get-tuple-element.566) | copy-start | bytes 786436
  50.3 6.8 %copy-start.3 = (f32[8,128,64]{2,1,0:T(8,128)}, f32[8,128,64]{2,1,0:T(8,128)S(1)}, u32[]{:S(2)}) copy-start(f32[8,128,64]{2,1,0:T(8,128)S(1)} %get-tuple-element.565) | copy-start | bytes 786436
  59.2 11.1 %collective-permute-start = (f32[4,1,8192]{2,1,0:T(1,128)}, f32[4,1,8192]{2,1,0:T(1,128)S(1)}, u32[]{:S(2)}, u32[]{:S(2)}) collective-permute-start(f32[4,1,8192]{2,1,0:T(1,128)} %get-tuple-element.552), channel_id=1, source_target_pairs={{16,0},{32,16},{48,32},{64,48},{80,64},{96,80},{112,96},{128,112},... | collective-permute-start | bytes 393224 | tf_op jit(solution)/shard_map/while/body/eval_jaxpr/ppermute | solution.py:26
  60.5 9.8 %collective-permute-start.1 = (f32[4,1,8192]{2,1,0:T(1,128)}, f32[4,1,8192]{2,1,0:T(1,128)}, u32[]{:S(2)}, u32[]{:S(2)}) collective-permute-start(f32[4,1,8192]{2,1,0:T(1,128)} %get-tuple-element.553), channel_id=1, source_target_pairs={{0,16},{16,32},{32,48},{48,64},{64,80},{80,96},{96,112},{112,128},... | collective-permute-start | bytes 393224 | tf_op jit(solution)/shard_map/while/body/eval_jaxpr/ppermute | solution.py:24
  78.7 11.7 %collective-permute-start = (f32[4,1,8192]{2,1,0:T(1,128)}, f32[4,1,8192]{2,1,0:T(1,128)S(1)}, u32[]{:S(2)}, u32[]{:S(2)}) collective-permute-start(f32[4,1,8192]{2,1,0:T(1,128)} %get-tuple-element.552), channel_id=1, source_target_pairs={{16,0},{32,16},{48,32},{64,48},{80,64},{96,80},{112,96},{128,112},... | collective-permute-start | bytes 393224 | tf_op jit(solution)/shard_map/while/body/eval_jaxpr/ppermute | solution.py:26
  80.0 10.4 %collective-permute-start.1 = (f32[4,1,8192]{2,1,0:T(1,128)}, f32[4,1,8192]{2,1,0:T(1,128)}, u32[]{:S(2)}, u32[]{:S(2)}) collective-permute-start(f32[4,1,8192]{2,1,0:T(1,128)} %get-tuple-element.553), channel_id=1, source_target_pairs={{0,16},{16,32},{32,48},{48,64},{64,80},{80,96},{96,112},{112,128},... | collective-permute-start | bytes 393224 | tf_op jit(solution)/shard_map/while/body/eval_jaxpr/ppermute | solution.py:24
  98.7 12.9 %collective-permute-start = (f32[4,1,8192]{2,1,0:T(1,128)}, f32[4,1,8192]{2,1,0:T(1,128)S(1)}, u32[]{:S(2)}, u32[]{:S(2)}) collective-permute-start(f32[4,1,8192]{2,1,0:T(1,128)} %get-tuple-element.552), channel_id=1, source_target_pairs={{16,0},{32,16},{48,32},{64,48},{80,64},{96,80},{112,96},{128,112},... | collective-permute-start | bytes 393224 | tf_op jit(solution)/shard_map/while/body/eval_jaxpr/ppermute | solution.py:26
  100.0 11.6 %collective-permute-start.1 = (f32[4,1,8192]{2,1,0:T(1,128)}, f32[4,1,8192]{2,1,0:T(1,128)}, u32[]{:S(2)}, u32[]{:S(2)}) collective-permute-start(f32[4,1,8192]{2,1,0:T(1,128)} %get-tuple-element.553), channel_id=1, source_target_pairs={{0,16},{16,32},{32,48},{48,64},{64,80},{80,96},{96,112},{112,128},... | collective-permute-start | bytes 393224 | tf_op jit(solution)/shard_map/while/body/eval_jaxpr/ppermute | solution.py:24
  119.9 12.2 %collective-permute-start = (f32[4,1,8192]{2,1,0:T(1,128)}, f32[4,1,8192]{2,1,0:T(1,128)S(1)}, u32[]{:S(2)}, u32[]{:S(2)}) collective-permute-start(f32[4,1,8192]{2,1,0:T(1,128)} %get-tuple-element.552), channel_id=1, source_target_pairs={{16,0},{32,16},{48,32},{64,48},{80,64},{96,80},{112,96},{128,112},... | collective-permute-start | bytes 393224 | tf_op jit(solution)/shard_map/while/body/eval_jaxpr/ppermute | solution.py:26
  121.2 11.0 %collective-permute-start.1 = (f32[4,1,8192]{2,1,0:T(1,128)}, f32[4,1,8192]{2,1,0:T(1,128)}, u32[]{:S(2)}, u32[]{:S(2)}) collective-permute-start(f32[4,1,8192]{2,1,0:T(1,128)} %get-tuple-element.553), channel_id=1, source_target_pairs={{0,16},{16,32},{32,48},{48,64},{64,80},{80,96},{96,112},{112,128},... | collective-permute-start | bytes 393224 | tf_op jit(solution)/shard_map/while/body/eval_jaxpr/ppermute | solution.py:24
  140.5 12.2 %collective-permute-start = (f32[4,1,8192]{2,1,0:T(1,128)}, f32[4,1,8192]{2,1,0:T(1,128)S(1)}, u32[]{:S(2)}, u32[]{:S(2)}) collective-permute-start(f32[4,1,8192]{2,1,0:T(1,128)} %get-tuple-element.552), channel_id=1, source_target_pairs={{16,0},{32,16},{48,32},{64,48},{80,64},{96,80},{112,96},{128,112},... | collective-permute-start | bytes 393224 | tf_op jit(solution)/shard_map/while/body/eval_jaxpr/ppermute | solution.py:26
  141.8 11.0 %collective-permute-start.1 = (f32[4,1,8192]{2,1,0:T(1,128)}, f32[4,1,8192]{2,1,0:T(1,128)}, u32[]{:S(2)}, u32[]{:S(2)}) collective-permute-start(f32[4,1,8192]{2,1,0:T(1,128)} %get-tuple-element.553), channel_id=1, source_target_pairs={{0,16},{16,32},{32,48},{48,64},{64,80},{80,96},{96,112},{112,128},... | collective-permute-start | bytes 393224 | tf_op jit(solution)/shard_map/while/body/eval_jaxpr/ppermute | solution.py:24
  161.1 12.2 %collective-permute-start = (f32[4,1,8192]{2,1,0:T(1,128)}, f32[4,1,8192]{2,1,0:T(1,128)S(1)}, u32[]{:S(2)}, u32[]{:S(2)}) collective-permute-start(f32[4,1,8192]{2,1,0:T(1,128)} %get-tuple-element.552), channel_id=1, source_target_pairs={{16,0},{32,16},{48,32},{64,48},{80,64},{96,80},{112,96},{128,112},... | collective-permute-start | bytes 393224 | tf_op jit(solution)/shard_map/while/body/eval_jaxpr/ppermute | solution.py:26
  162.4 11.0 %collective-permute-start.1 = (f32[4,1,8192]{2,1,0:T(1,128)}, f32[4,1,8192]{2,1,0:T(1,128)}, u32[]{:S(2)}, u32[]{:S(2)}) collective-permute-start(f32[4,1,8192]{2,1,0:T(1,128)} %get-tuple-element.553), channel_id=1, source_target_pairs={{0,16},{16,32},{32,48},{48,64},{64,80},{80,96},{96,112},{112,128},... | collective-permute-start | bytes 393224 | tf_op jit(solution)/shard_map/while/body/eval_jaxpr/ppermute | solution.py:24
  181.7 12.2 %collective-permute-start = (f32[4,1,8192]{2,1,0:T(1,128)}, f32[4,1,8192]{2,1,0:T(1,128)S(1)}, u32[]{:S(2)}, u32[]{:S(2)}) collective-permute-start(f32[4,1,8192]{2,1,0:T(1,128)} %get-tuple-element.552), channel_id=1, source_target_pairs={{16,0},{32,16},{48,32},{64,48},{80,64},{96,80},{112,96},{128,112},... | collective-permute-start | bytes 393224 | tf_op jit(solution)/shard_map/while/body/eval_jaxpr/ppermute | solution.py:26
  183.0 11.0 %collective-permute-start.1 = (f32[4,1,8192]{2,1,0:T(1,128)}, f32[4,1,8192]{2,1,0:T(1,128)}, u32[]{:S(2)}, u32[]{:S(2)}) collective-permute-start(f32[4,1,8192]{2,1,0:T(1,128)} %get-tuple-element.553), channel_id=1, source_target_pairs={{0,16},{16,32},{32,48},{48,64},{64,80},{80,96},{96,112},{112,128},... | collective-permute-start | bytes 393224 | tf_op jit(solution)/shard_map/while/body/eval_jaxpr/ppermute | solution.py:24
  202.3 12.2 %collective-permute-start = (f32[4,1,8192]{2,1,0:T(1,128)}, f32[4,1,8192]{2,1,0:T(1,128)S(1)}, u32[]{:S(2)}, u32[]{:S(2)}) collective-permute-start(f32[4,1,8192]{2,1,0:T(1,128)} %get-tuple-element.552), channel_id=1, source_target_pairs={{16,0},{32,16},{48,32},{64,48},{80,64},{96,80},{112,96},{128,112},... | collective-permute-start | bytes 393224 | tf_op jit(solution)/shard_map/while/body/eval_jaxpr/ppermute | solution.py:26
  203.6 11.0 %collective-permute-start.1 = (f32[4,1,8192]{2,1,0:T(1,128)}, f32[4,1,8192]{2,1,0:T(1,128)}, u32[]{:S(2)}, u32[]{:S(2)}) collective-permute-start(f32[4,1,8192]{2,1,0:T(1,128)} %get-tuple-element.553), channel_id=1, source_target_pairs={{0,16},{16,32},{32,48},{48,64},{64,80},{80,96},{96,112},{112,128},... | collective-permute-start | bytes 393224 | tf_op jit(solution)/shard_map/while/body/eval_jaxpr/ppermute | solution.py:24
  222.9 12.2 %collective-permute-start = (f32[4,1,8192]{2,1,0:T(1,128)}, f32[4,1,8192]{2,1,0:T(1,128)S(1)}, u32[]{:S(2)}, u32[]{:S(2)}) collective-permute-start(f32[4,1,8192]{2,1,0:T(1,128)} %get-tuple-element.552), channel_id=1, source_target_pairs={{16,0},{32,16},{48,32},{64,48},{80,64},{96,80},{112,96},{128,112},... | collective-permute-start | bytes 393224 | tf_op jit(solution)/shard_map/while/body/eval_jaxpr/ppermute | solution.py:26
  224.2 11.0 %collective-permute-start.1 = (f32[4,1,8192]{2,1,0:T(1,128)}, f32[4,1,8192]{2,1,0:T(1,128)}, u32[]{:S(2)}, u32[]{:S(2)}) collective-permute-start(f32[4,1,8192]{2,1,0:T(1,128)} %get-tuple-element.553), channel_id=1, source_target_pairs={{0,16},{16,32},{32,48},{48,64},{64,80},{80,96},{96,112},{112,128},... | collective-permute-start | bytes 393224 | tf_op jit(solution)/shard_map/while/body/eval_jaxpr/ppermute | solution.py:24
  243.5 12.2 %collective-permute-start = (f32[4,1,8192]{2,1,0:T(1,128)}, f32[4,1,8192]{2,1,0:T(1,128)S(1)}, u32[]{:S(2)}, u32[]{:S(2)}) collective-permute-start(f32[4,1,8192]{2,1,0:T(1,128)} %get-tuple-element.552), channel_id=1, source_target_pairs={{16,0},{32,16},{48,32},{64,48},{80,64},{96,80},{112,96},{128,112},... | collective-permute-start | bytes 393224 | tf_op jit(solution)/shard_map/while/body/eval_jaxpr/ppermute | solution.py:26
  244.8 11.0 %collective-permute-start.1 = (f32[4,1,8192]{2,1,0:T(1,128)}, f32[4,1,8192]{2,1,0:T(1,128)}, u32[]{:S(2)}, u32[]{:S(2)}) collective-permute-start(f32[4,1,8192]{2,1,0:T(1,128)} %get-tuple-element.553), channel_id=1, source_target_pairs={{0,16},{16,32},{32,48},{48,64},{64,80},{80,96},{96,112},{112,128},... | collective-permute-start | bytes 393224 | tf_op jit(solution)/shard_map/while/body/eval_jaxpr/ppermute | solution.py:24
  264.1 12.3 %collective-permute-start = (f32[4,1,8192]{2,1,0:T(1,128)}, f32[4,1,8192]{2,1,0:T(1,128)S(1)}, u32[]{:S(2)}, u32[]{:S(2)}) collective-permute-start(f32[4,1,8192]{2,1,0:T(1,128)} %get-tuple-element.552), channel_id=1, source_target_pairs={{16,0},{32,16},{48,32},{64,48},{80,64},{96,80},{112,96},{128,112},... | collective-permute-start | bytes 393224 | tf_op jit(solution)/shard_map/while/body/eval_jaxpr/ppermute | solution.py:26
  265.4 11.1 %collective-permute-start.1 = (f32[4,1,8192]{2,1,0:T(1,128)}, f32[4,1,8192]{2,1,0:T(1,128)}, u32[]{:S(2)}, u32[]{:S(2)}) collective-permute-start(f32[4,1,8192]{2,1,0:T(1,128)} %get-tuple-element.553), channel_id=1, source_target_pairs={{0,16},{16,32},{32,48},{48,64},{64,80},{80,96},{96,112},{112,128},... | collective-permute-start | bytes 393224 | tf_op jit(solution)/shard_map/while/body/eval_jaxpr/ppermute | solution.py:24
  284.8 13.1 %collective-permute-start = (f32[4,1,8192]{2,1,0:T(1,128)}, f32[4,1,8192]{2,1,0:T(1,128)S(1)}, u32[]{:S(2)}, u32[]{:S(2)}) collective-permute-start(f32[4,1,8192]{2,1,0:T(1,128)} %get-tuple-element.552), channel_id=1, source_target_pairs={{16,0},{32,16},{48,32},{64,48},{80,64},{96,80},{112,96},{128,112},... | collective-permute-start | bytes 393224 | tf_op jit(solution)/shard_map/while/body/eval_jaxpr/ppermute | solution.py:26
  286.1 11.9 %collective-permute-start.1 = (f32[4,1,8192]{2,1,0:T(1,128)}, f32[4,1,8192]{2,1,0:T(1,128)}, u32[]{:S(2)}, u32[]{:S(2)}) collective-permute-start(f32[4,1,8192]{2,1,0:T(1,128)} %get-tuple-element.553), channel_id=1, source_target_pairs={{0,16},{16,32},{32,48},{48,64},{64,80},{80,96},{96,112},{112,128},... | collective-permute-start | bytes 393224 | tf_op jit(solution)/shard_map/while/body/eval_jaxpr/ppermute | solution.py:24
  306.3 13.1 %collective-permute-start = (f32[4,1,8192]{2,1,0:T(1,128)}, f32[4,1,8192]{2,1,0:T(1,128)S(1)}, u32[]{:S(2)}, u32[]{:S(2)}) collective-permute-start(f32[4,1,8192]{2,1,0:T(1,128)} %get-tuple-element.552), channel_id=1, source_target_pairs={{16,0},{32,16},{48,32},{64,48},{80,64},{96,80},{112,96},{128,112},... | collective-permute-start | bytes 393224 | tf_op jit(solution)/shard_map/while/body/eval_jaxpr/ppermute | solution.py:26
  307.6 11.9 %collective-permute-start.1 = (f32[4,1,8192]{2,1,0:T(1,128)}, f32[4,1,8192]{2,1,0:T(1,128)}, u32[]{:S(2)}, u32[]{:S(2)}) collective-permute-start(f32[4,1,8192]{2,1,0:T(1,128)} %get-tuple-element.553), channel_id=1, source_target_pairs={{0,16},{16,32},{32,48},{48,64},{64,80},{80,96},{96,112},{112,128},... | collective-permute-start | bytes 393224 | tf_op jit(solution)/shard_map/while/body/eval_jaxpr/ppermute | solution.py:24
  327.8 13.1 %collective-permute-start = (f32[4,1,8192]{2,1,0:T(1,128)}, f32[4,1,8192]{2,1,0:T(1,128)S(1)}, u32[]{:S(2)}, u32[]{:S(2)}) collective-permute-start(f32[4,1,8192]{2,1,0:T(1,128)} %get-tuple-element.552), channel_id=1, source_target_pairs={{16,0},{32,16},{48,32},{64,48},{80,64},{96,80},{112,96},{128,112},... | collective-permute-start | bytes 393224 | tf_op jit(solution)/shard_map/while/body/eval_jaxpr/ppermute | solution.py:26
  329.1 11.9 %collective-permute-start.1 = (f32[4,1,8192]{2,1,0:T(1,128)}, f32[4,1,8192]{2,1,0:T(1,128)}, u32[]{:S(2)}, u32[]{:S(2)}) collective-permute-start(f32[4,1,8192]{2,1,0:T(1,128)} %get-tuple-element.553), channel_id=1, source_target_pairs={{0,16},{16,32},{32,48},{48,64},{64,80},{80,96},{96,112},{112,128},... | collective-permute-start | bytes 393224 | tf_op jit(solution)/shard_map/while/body/eval_jaxpr/ppermute | solution.py:24
  349.3 13.1 %collective-permute-start = (f32[4,1,8192]{2,1,0:T(1,128)}, f32[4,1,8192]{2,1,0:T(1,128)S(1)}, u32[]{:S(2)}, u32[]{:S(2)}) collective-permute-start(f32[4,1,8192]{2,1,0:T(1,128)} %get-tuple-element.552), channel_id=1, source_target_pairs={{16,0},{32,16},{48,32},{64,48},{80,64},{96,80},{112,96},{128,112},... | collective-permute-start | bytes 393224 | tf_op jit(solution)/shard_map/while/body/eval_jaxpr/ppermute | solution.py:26
  350.6 11.9 %collective-permute-start.1 = (f32[4,1,8192]{2,1,0:T(1,128)}, f32[4,1,8192]{2,1,0:T(1,128)}, u32[]{:S(2)}, u32[]{:S(2)}) collective-permute-start(f32[4,1,8192]{2,1,0:T(1,128)} %get-tuple-element.553), channel_id=1, source_target_pairs={{0,16},{16,32},{32,48},{48,64},{64,80},{80,96},{96,112},{112,128},... | collective-permute-start | bytes 393224 | tf_op jit(solution)/shard_map/while/body/eval_jaxpr/ppermute | solution.py:24
  370.8 13.1 %collective-permute-start = (f32[4,1,8192]{2,1,0:T(1,128)}, f32[4,1,8192]{2,1,0:T(1,128)S(1)}, u32[]{:S(2)}, u32[]{:S(2)}) collective-permute-start(f32[4,1,8192]{2,1,0:T(1,128)} %get-tuple-element.552), channel_id=1, source_target_pairs={{16,0},{32,16},{48,32},{64,48},{80,64},{96,80},{112,96},{128,112},... | collective-permute-start | bytes 393224 | tf_op jit(solution)/shard_map/while/body/eval_jaxpr/ppermute | solution.py:26
  372.1 11.9 %collective-permute-start.1 = (f32[4,1,8192]{2,1,0:T(1,128)}, f32[4,1,8192]{2,1,0:T(1,128)}, u32[]{:S(2)}, u32[]{:S(2)}) collective-permute-start(f32[4,1,8192]{2,1,0:T(1,128)} %get-tuple-element.553), channel_id=1, source_target_pairs={{0,16},{16,32},{32,48},{48,64},{64,80},{80,96},{96,112},{112,128},... | collective-permute-start | bytes 393224 | tf_op jit(solution)/shard_map/while/body/eval_jaxpr/ppermute | solution.py:24
where the time goes:
time: 571 us; the launch traced here: 567 us
  other arithmetic  172 us (30%)
  blocking collectives  159 us (28%)
  local copies, waits for them, and re-layouts  117 us (20%)
  starting transfers between devices  115 us (20%)
    psum x1, blocking collectives, on_device(): gram = lax.psum(gram_part, ('space', 'probe'))  115 us
    add x16, other arithmetic, single(): search = table[step, 0] * search + table[step, 1] * resid  100 us
    ppermute x17, starting transfers between devices, padded_2(): lax.ppermute(tail, axis, [(i, (i + 1) % count) for i in range(ends)])  93.6 us
    all_to_all x1, blocking collectives, on_device(): lax.all_to_all(flat_fields, 'probe', split_axis=1, concat_axis=0, tiled=T...  43.9 us
    add x16, other arithmetic, single(): iterate = iterate + search  35.6 us
    slice x16, local copies, waits for them, and re-layouts, apply_operator(): below_y = jnp.concatenate([zeros_y, centre[..., :-layer]], -1)  26.4 us
    dynamic_slice x16, local copies, waits for them, and re-layouts, single(): search = table[step, 0] * search + table[step, 1] * resid  22.8 us
    ppermute x17, starting transfers between devices, padded_2(): lax.ppermute(head, axis, [((i + 1) % count, i) for i in range(ends)])  21.8 us
  transfers between devices with their start and end apart: 34, of which 0 were waited for; matrix products, arithmetic and copies ran while one was open for 24% of the time, Pallas kernels for 0%

commit v1 on v0

v1 whole, which is shorter than its diff:
```python
import functools
import math

import jax
import jax.numpy as jnp
from jax import lax
from jax.experimental import pallas as pl
from jax.experimental.pallas import tpu as pltpu
from jax.sharding import PartitionSpec as P

NZ = 64
SWEEPS = 16
REACH = 2
SPAN = 2 * REACH + 1
GROUP = 16
CHIPS = 8
SLOTS = GROUP * SPAN
QUADS = 8
PAIRS = 32
PAD = 16

bound_low = 0.005
bound_high = 24.5

F32 = jnp.float32
VMEM = pltpu.VMEM
SMEM = pltpu.SMEM


def chebyshev_table(count):
    center = 0.5 * (bound_high + bound_low)
    spread = 0.5 * (bound_high - bound_low)
    ratio = center / spread
    rho_prev = 1.0 / ratio
    entries = []
    for index_step in range(count):
        rho_next = 1.0 / (2.0 * ratio - rho_prev)
        entries.append((rho_next * rho_prev, 2.0 * rho_next / spread))
        rho_prev = rho_next
    return entries


def start_scale():
    return 1.0 / (0.5 * (bound_high + bound_low))


def decode(cell):
    cell = jnp.maximum(cell, 0)
    x = lax.shift_right_logical(cell, 13)
    y = lax.bitwise_and(lax.shift_right_logical(cell, 6), 127)
    z = lax.bitwise_and(cell, 63)
    y_first = lax.bitwise_and(y + 1, 126 + 128) - 16
    return x, y, y_first, z, z - 15


def lanes(shape=(8, 128)):
    return lax.broadcasted_iota(jnp.int32, shape, 1)


def sublanes(shape=(8, 128)):
    return lax.broadcasted_iota(jnp.int32, shape, 0)


def wrap(shift):
    return lax.bitwise_and(shift, 127)


def cut_kernel(cell_ref, cond_ref, leak_ref, out_ref):
    me = lax.axis_index("probe")
    chip = me // 2
    core = me % 2
    lane = lanes()
    for e in range(SPAN):
        _, _, y_first, _, z_first = decode(cell_ref[core, chip * SPAN + e])
        pair_first = y_first // 2
        shifts = [wrap(128 - z_first), wrap(96 - z_first), wrap(64 - z_first + 128), wrap(32 - z_first + 128)]
        for k in range(QUADS):
            one = pl.multiple_of(jnp.clip(pair_first + 2 * k, 0, 63) * 128, 128)
            two = pl.multiple_of(jnp.clip(pair_first + 2 * k + 1, 0, 63) * 128, 128)
            for prop, ref in enumerate((cond_ref, leak_ref)):
                a = ref[:, pl.ds(one, 128)]
                b = ref[:, pl.ds(two, 128)]
                low = jnp.where(lane < 32, pltpu.roll(a, shifts[0], 1), pltpu.roll(a, shifts[1], 1))
                high = jnp.where(lane < 96, pltpu.roll(b, shifts[2], 1), pltpu.roll(b, shifts[3], 1))
                out_ref[e, prop, k] = jnp.where(lane < 64, low, high)


def barrier_with(partners):
    barrier = pltpu.get_barrier_semaphore()
    for partner in partners:
        pl.semaphore_signal(barrier, inc=1, device_id=partner, device_id_type=pl.DeviceIdType.MESH)
    pl.semaphore_wait(barrier, len(partners))


def remote(src, dst, send, recv, device):
    return pltpu.make_async_remote_copy(
        src_ref=src, dst_ref=dst, send_sem=send, recv_sem=recv, device_id=device, device_id_type=pl.DeviceIdType.MESH
    )


OFFSETS = (-2, -1, 1, 2)


def window_kernel(own_ref, signs_ref, win_ref, sign_out, send_sem, recv_sem, sign_send, sign_recv, pair_sem):
    count = lax.axis_size("space")
    here = lax.axis_index("space")
    me = lax.axis_index("probe")
    chip = me // 2
    core = me % 2
    near = [(lax.rem(here + d + count, count), me) for d in OFFSETS]
    along = [(here, lax.rem(chip + r, CHIPS) * 2 + core) for r in range(1, CHIPS)]
    twin = (here, chip * 2 + 1 - core)
    barrier_with(near + along + [twin])
    copies = []
    for i, d in enumerate(OFFSETS):
        copies.append(remote(own_ref.at[d + 2], win_ref.at[2 - d], send_sem.at[i], recv_sem.at[i], near[i]))
        copies[-1].start()
    signs = []
    for r in range(1, CHIPS):
        signs.append(remote(signs_ref, sign_out.at[core, chip], sign_send.at[r], sign_recv.at[r], along[r - 1]))
        signs[-1].start()
    win_ref[REACH] = own_ref[REACH]
    sign_out[core, chip] = signs_ref[...]
    for copy in signs:
        copy.wait()
    pair = remote(sign_out.at[core], sign_out.at[core], pair_sem.at[0], pair_sem.at[1], twin)
    pair.start()
    pair.wait()
    for copy in copies:
        copy.wait()


def shifted(own, before, after, lane_group, sub):
    down = pltpu.roll(own, 1, 0)
    up = pltpu.roll(own, 7, 0)
    return down, up


def solve_kernel(cell_ref, win_ref, out_ref, coef, search, resid, total):
    here = lax.axis_index("space")
    me = lax.axis_index("probe")
    chip = me // 2
    core = me % 2
    cell = cell_ref[core, chip * SPAN + REACH]
    x, y, y_first, z, z_first = decode(cell)
    lane = lanes()
    sub = sublanes()
    group = lane // 32
    depth = lane % 32
    zz = z_first + depth
    z_ok = (zz >= 0) & (zz < NZ)
    zm_ok = z_ok & (zz >= 1)
    zp_ok = z_ok & (zz < NZ - 1)
    weight = jnp.where(cell >= 0, 1.0, 0.0).astype(F32)

    for b in range(SPAN):
        xx = (here + (b - REACH)) * 8 + sub
        x_ok = (xx >= 0) & (xx < 256)
        xm_in = xx >= 1
        xp_in = xx < 255
        for k in range(QUADS):
            yy = y_first + 4 * k + group
            y_ok = (yy >= 0) & (yy < 128)
            inside = x_ok & y_ok & z_ok
            own = win_ref[b, 0, k]
            before = win_ref[max(b - 1, 0), 0, k]
            after = win_ref[min(b + 1, SPAN - 1), 0, k]
            left = win_ref[b, 0, max(k - 1, 0)]
            right = win_ref[b, 0, min(k + 1, QUADS - 1)]
            parts = (
                (jnp.where(sub == 0, pltpu.roll(before, 1, 0), pltpu.roll(own, 1, 0)), xm_in),
                (jnp.where(sub == 7, pltpu.roll(after, 7, 0), pltpu.roll(own, 7, 0)), xp_in),
                (jnp.where(group == 0, pltpu.roll(left, 32, 1), pltpu.roll(own, 32, 1)), yy >= 1),
                (jnp.where(group == 3, pltpu.roll(right, 96, 1), pltpu.roll(own, 96, 1)), yy < 127),
                (pltpu.roll(own, 1, 1), zz >= 1),
                (pltpu.roll(own, 127, 1), zz < NZ - 1),
            )
            diagonal = win_ref[b, 1, k]
            for n, (other, there) in enumerate(parts):
                face = 0.5 * (own + jnp.where(there, other, own))
                diagonal = diagonal + face
                coef[n + 1, b, k] = jnp.where(inside & there, face, 0.0)
            coef[0, b, k] = diagonal

    zero = jnp.zeros((8, 128), F32)
    x_in = x - here * 8
    for b in range(SPAN):
        for k in range(QUADS):
            search[1, b, k] = zero
            if b == REACH and k in (3, 4):
                hit = (sub == x_in) & (4 * k + group == y - y_first) & (depth == 15)
                source = jnp.where(hit, weight, 0.0)
                resid[b, k] = source
                search[0, b, k] = source * start_scale()
            else:
                resid[b, k] = zero
                search[0, b, k] = zero
            total[b, k] = zero

    table = chebyshev_table(SWEEPS)
    for j in range(SWEEPS - 1):
        a, c = (float(value) for value in table[j])
        now, later = j % 2, (j + 1) % 2
        wide = j + 1
        k_low, k_high = (15 - wide) // 4, (16 + wide) // 4
        b_low, b_high = (1, 3) if wide <= 8 else (0, 4)
        for b in range(b_low, b_high + 1):
            for k in range(k_low, k_high + 1):
                own = search[now, b, k]
                down = pltpu.roll(own, 1, 0)
                up = pltpu.roll(own, 7, 0)
                edge = pltpu.roll(search[now, b - 1, k], 1, 0) if b > 0 else zero
                down = jnp.where(sub == 0, edge, down)
                edge = pltpu.roll(search[now, b + 1, k], 7, 0) if b < SPAN - 1 else zero
                up = jnp.where(sub == 7, edge, up)
                edge = pltpu.roll(search[now, b, k - 1], 32, 1) if k > 0 else zero
                left = jnp.where(group == 0, edge, pltpu.roll(own, 32, 1))
                edge = pltpu.roll(search[now, b, k + 1], 96, 1) if k < QUADS - 1 else zero
                right = jnp.where(group == 3, edge, pltpu.roll(own, 96, 1))
                image = coef[0, b, k] * own
                image = image - coef[1, b, k] * down
                image = image - coef[2, b, k] * up
                image = image - coef[3, b, k] * left
                image = image - coef[4, b, k] * right
                image = image - coef[5, b, k] * pltpu.roll(own, 1, 1)
                image = image - coef[6, b, k] * pltpu.roll(own, 127, 1)
                rest = resid[b, k] - image
                resid[b, k] = rest
                total[b, k] = total[b, k] + own
                search[later, b, k] = a * own + c * rest
    last = (SWEEPS - 1) % 2
    for b in range(SPAN):
        for k in range(QUADS):
            total[b, k] = total[b, k] + search[last, b, k]
    for b in range(SPAN):
        for r in range(8):
            out_ref[b, r] = total[b, :, r, :]


def spread_kernel(own_ref, out_ref, block_ref, send_sem, recv_sem, row_send, row_recv, pair_send, pair_recv):
    count = lax.axis_size("space")
    here = lax.axis_index("space")
    me = lax.axis_index("probe")
    chip = me // 2
    core = me % 2
    near = [(lax.rem(here + d + count, count), me) for d in OFFSETS]
    along = [(here, lax.rem(chip + r, CHIPS) * 2 + core) for r in range(1, CHIPS)]
    twin = (here, chip * 2 + 1 - core)
    barrier_with(near + along + [twin])
    copies = []
    for i, d in enumerate(OFFSETS):
        copies.append(remote(own_ref.at[d + 2], block_ref.at[2 - d], send_sem.at[i], recv_sem.at[i], near[i]))
        copies[-1].start()
    block_ref[REACH] = own_ref[REACH]
    for copy in copies:
        copy.wait()
    rows = []
    for r in range(1, CHIPS):
        target = lax.rem(chip + r, CHIPS)
        rows.append(
            remote(block_ref.at[:, target], out_ref.at[core, chip], row_send.at[r], row_recv.at[r], along[r - 1])
        )
        rows[-1].start()
    out_ref[core, chip] = block_ref[:, chip]
    pairs = []
    for r in range(CHIPS):
        source = lax.rem(chip - r + CHIPS, CHIPS)
        if r:
            rows[r - 1].wait_recv()
        part = out_ref.at[core, source]
        pairs.append(remote(part, part, pair_send.at[r], pair_recv.at[r], twin))
        pairs[-1].start()
    for copy in rows:
        copy.wait_send()
    for copy in pairs:
        copy.wait()


def split3(value):
    high = value.astype(jnp.bfloat16)
    rest = value - high.astype(F32)
    mid = rest.astype(jnp.bfloat16)
    low = (rest - mid.astype(F32)).astype(jnp.bfloat16)
    return high, mid, low


def place_kernel(turn_ref, cell_ref, part_ref, slot_ref, signs_ref, before_ref, out_ref, gram_ref, placed):
    half = lax.axis_index("probe") % 2
    lane = lanes()

    def clear(i, _):
        placed[pl.ds(pl.multiple_of(i * 64, 64), 64), :] = jnp.zeros((64, 128), F32)
        return 0

    lax.fori_loop(0, (PAIRS + 2 * PAD) * SLOTS // 64, clear, 0)

    def place(n, _):
        for c in range(2):
            _, _, y_first, _, z_first = decode(cell_ref[c, n])
            first = jnp.clip(y_first // 2 - PAIRS * half, -PAD, PAIRS) + PAD
            own = part_ref[c, n]
            shift = lane - z_first
            even = (shift >= 0) & (shift < 32) & (lane < 64)
            odd = (shift >= 64) & (shift < 96) & (lane >= 64)
            for m in range(2):
                row = jnp.where(even, pltpu.roll(own, wrap(z_first - 64 * m + 256), 1), 0.0)
                row = jnp.where(odd, pltpu.roll(own, wrap(z_first + 32 - 64 * m + 256), 1), row)
                start = (first + m) * SLOTS + c * (SLOTS // 2) + n
                placed[pl.ds(start, 8, stride=2 * SLOTS), :] = row
        return 0

    lax.fori_loop(0, SLOTS // 2, place, 0)

    table = jnp.concatenate([signs_ref[p % 2, p // 2] for p in range(GROUP)], axis=0)
    table = (2 * table - 1).astype(jnp.bfloat16)
    which = lax.broadcasted_iota(jnp.int32, (256, 128), 0) == slot_ref[...]
    pick = jnp.dot(table, which.astype(jnp.bfloat16), preferred_element_type=F32)
    pick = pick[:, :SLOTS].astype(jnp.bfloat16)
    pick = jnp.concatenate([pick, pick, pick], axis=1)
    first_turn = turn_ref[0] == 0
    gram = jnp.zeros((64, 64), F32)
    for t in range(PAIRS):
        base = (t + PAD) * SLOTS
        value = jnp.concatenate(split3(placed[base : base + SLOTS, :]), axis=0)
        value = jnp.dot(pick, value, preferred_element_type=F32)
        value = value + jnp.where(first_turn, 0.0, before_ref[:, 128 * t : 128 * t + 128])
        out_ref[:, 128 * t : 128 * t + 128] = value
    sketch = out_ref[...]
    gram = lax.dot_general(
        sketch, sketch, (((1,), (1,)), ((), ())), precision=lax.Precision.HIGHEST, preferred_element_type=F32
    )
    gram = jnp.concatenate([gram, jnp.zeros((64, 64), F32)], axis=1)
    for p in range(GROUP):
        gram_ref[p] = gram[4 * p : 4 * p + 4]


def sum_kernel(part_ref, out_ref, got, z_buf, x_buf, s1, r1, s2, r2, s3, r3, s4, r4):
    here = lax.axis_index("space")
    me = lax.axis_index("probe")
    x = here // 8
    z = here % 8
    group = [(here, lax.rem(me + r, GROUP)) for r in range(1, GROUP)]
    ring_z = [(x * 8 + lax.rem(z + r, 8), me) for r in range(1, 8)]
    ring_x = [(lax.rem(x + r, 4) * 8 + z, me) for r in range(1, 4)]
    barrier_with(group + ring_z + ring_x)
    copies = []
    for r in range(1, GROUP):
        copies.append(remote(part_ref.at[lax.rem(me + r, GROUP)], got.at[r], s1.at[r], r1.at[r], group[r - 1]))
        copies[-1].start()
    value = part_ref[me]
    for r in range(1, GROUP):
        copies[r - 1].wait_recv()
    got[0] = value
    total = got[0]
    for r in range(1, GROUP):
        total = total + got[r]
    z_buf[z] = total
    steps = []
    for r in range(1, 8):
        steps.append(remote(z_buf.at[z], z_buf.at[z], s2.at[r], r2.at[r], ring_z[r - 1]))
        steps[-1].start()
    for copy in steps:
        copy.wait_recv()
    total = z_buf[0]
    for r in range(1, 8):
        total = total + z_buf[r]
    x_buf[x] = total
    turns = []
    for r in range(1, 4):
        turns.append(remote(x_buf.at[x], x_buf.at[x], s3.at[r], r3.at[r], ring_x[r - 1]))
        turns[-1].start()
    for copy in turns:
        copy.wait_recv()
    total = ((x_buf[0] + x_buf[1]) + x_buf[2]) + x_buf[3]
    out_ref[me] = total
    last = []
    for r in range(1, GROUP):
        last.append(remote(out_ref.at[me], out_ref.at[me], s4.at[r], r4.at[r], group[r - 1]))
        last[-1].start()
    for copy in copies + steps + turns:
        copy.wait_send()
    for copy in last:
        copy.wait()


def finish_kernel(gram_ref, sketch_ref, basis_ref, factor_ref):
    shape = (8, 128)
    lane = lanes(shape)
    sub = sublanes(shape)
    rows = []
    for i in range(8):
        block = jnp.concatenate([gram_ref[2 * i], gram_ref[2 * i + 1]], axis=0)
        rows.append(jnp.where(lane - 64 == sub + 8 * i, 1.0, block))
    for k in range(64):
        owner, inner = k // 8, k % 8
        row = jnp.broadcast_to(rows[owner][inner : inner + 1, :], shape)
        pivot = jnp.broadcast_to(row[:, k : k + 1], shape)
        scale = lax.rsqrt(pivot)
        scale = scale * (1.5 - 0.5 * pivot * scale * scale)
        row = row * scale
        for i in range(owner, 8):
            many = jnp.broadcast_to(rows[i][:, k : k + 1], shape) * scale
            fresh = rows[i] - many * row
            if i == owner:
                fresh = jnp.where(sub > inner, fresh, jnp.where(sub == inner, row, rows[i]))
            rows[i] = fresh
    full = jnp.concatenate(rows, axis=0)
    row_at = lax.broadcasted_iota(jnp.int32, (64, 64), 0)
    col_at = lax.broadcasted_iota(jnp.int32, (64, 64), 1)
    upper = jnp.where(col_at >= row_at, full[:, :64], 0.0)
    factor_ref[...] = upper * (1.0 / math.sqrt(256))
    inverse = full[:, 64:] * math.sqrt(256 * 128 * 64)
    basis_ref[...] = jnp.dot(
        inverse, sketch_ref[...], precision=lax.Precision.HIGHEST, preferred_element_type=F32
    )


def params(**more):
    return pltpu.CompilerParams(vmem_limit_bytes=48 * 1024 * 1024, **more)


def whole(space=VMEM):
    return pl.BlockSpec(memory_space=space)


def dma(*shape):
    return pltpu.SemaphoreType.DMA(shape)


def on_device(conductivity, leakage, signs, wells):
    here = lax.axis_index("space")
    cells = conductivity.shape[0] * conductivity.shape[1]
    probes = signs.shape[0] * GROUP
    count = wells.shape[0]
    owner = wells // cells
    index = jnp.arange(count, dtype=jnp.int32)
    rank = jnp.sum((owner[None, :] == owner[:, None]) & (index[None, :] < index[:, None]), axis=1, dtype=jnp.int32)
    rounds = jnp.max(rank) // GROUP + 1
    slot = jnp.arange(SLOTS, dtype=jnp.int32)
    slot_probe = (slot % (SLOTS // 2)) // SPAN * 2 + slot // (SLOTS // 2)
    slot_block = here + slot % SPAN - REACH

    def body(carry):
        turn, sketch, _ = carry
        match = (owner[None, :] == slot_block[:, None]) & (rank[None, :] == turn * GROUP + slot_probe[:, None])
        chosen = jnp.max(jnp.where(match, index[None, :], -1), axis=1)
        cell = jnp.max(jnp.where(match, wells[None, :], -1), axis=1).reshape(2, SLOTS // 2)
        chosen = jnp.concatenate([chosen, jnp.full((128 - SLOTS,), -1, jnp.int32)])[None, :]
        windows = pl.pallas_call(
            cut_kernel,
            out_shape=jax.ShapeDtypeStruct((SPAN, 2, QUADS, 8, 128), F32),
            in_specs=[whole(SMEM), whole(), whole()],
            out_specs=whole(),
            compiler_params=params(),
            name="cut",
        )(cell, conductivity, leakage)
        windows, all_signs = pl.pallas_call(
            window_kernel,
            out_shape=(
                jax.ShapeDtypeStruct((SPAN, 2, QUADS, 8, 128), F32),
                jax.ShapeDtypeStruct((2, CHIPS, probes // GROUP, count), jnp.int32),
            ),
            in_specs=[whole(), whole()],
            out_specs=(whole(), whole()),
            scratch_shapes=[dma(4), dma(4), dma(8), dma(8), dma(2)],
            compiler_params=params(collective_id=0, has_side_effects=True),
            name="windows",
        )(windows, signs)
        fields = pl.pallas_call(
            solve_kernel,
            out_shape=jax.ShapeDtypeStruct((SPAN, 8, QUADS, 128), F32),
            in_specs=[whole(SMEM), whole()],
            out_specs=whole(),
            scratch_shapes=[
                VMEM((7, SPAN, QUADS, 8, 128), F32),
                VMEM((2, SPAN, QUADS, 8, 128), F32),
                VMEM((SPAN, QUADS, 8, 128), F32),
                VMEM((SPAN, QUADS, 8, 128), F32),
            ],
            compiler_params=params(),
            name="solve",
        )(cell, windows)
        fields = pl.pallas_call(
            spread_kernel,
            out_shape=jax.ShapeDtypeStruct((2, CHIPS, SPAN, QUADS, 128), F32),
            in_specs=[whole()],
            out_specs=whole(),
            scratch_shapes=[VMEM((SPAN, 8, QUADS, 128), F32), dma(4), dma(4), dma(8), dma(8), dma(8), dma(8)],
            compiler_params=params(collective_id=1, has_side_effects=True),
            name="spread",
        )(fields)
        sketch, gram = pl.pallas_call(
            place_kernel,
            out_shape=(
                jax.ShapeDtypeStruct(sketch.shape, F32),
                jax.ShapeDtypeStruct((GROUP, 4, 128), F32),
            ),
            in_specs=[whole(SMEM), whole(SMEM), whole(), whole(), whole(), whole()],
            out_specs=(whole(), whole()),
            scratch_shapes=[VMEM(((PAIRS + 2 * PAD) * SLOTS, 128), F32)],
            compiler_params=params(),
            name="place",
        )(turn.reshape(1), cell, fields.reshape(2, SLOTS // 2, QUADS, 128), chosen, all_signs, sketch)
        return turn + 1, sketch, gram

    sketch = jnp.zeros((probes, cells // GROUP), F32)
    gram = jnp.zeros((GROUP, 4, 128), F32)
    _, sketch, gram = lax.while_loop(lambda carry: carry[0] < rounds, body, (jnp.int32(0), sketch, gram))
    gram = pl.pallas_call(
        sum_kernel,
        out_shape=jax.ShapeDtypeStruct((GROUP, 4, 128), F32),
        in_specs=[whole()],
        out_specs=whole(),
        scratch_shapes=[
            VMEM((GROUP, 4, 128), F32),
            VMEM((8, 4, 128), F32),
            VMEM((4, 4, 128), F32),
            dma(GROUP),
            dma(GROUP),
            dma(8),
            dma(8),
            dma(4),
            dma(4),
            dma(GROUP),
            dma(GROUP),
        ],
        compiler_params=params(collective_id=2, has_side_effects=True),
        name="gram_sum",
    )(gram)
    return pl.pallas_call(
        finish_kernel,
        out_shape=(
            jax.ShapeDtypeStruct((probes, cells // GROUP), F32),
            jax.ShapeDtypeStruct((probes, probes), F32),
        ),
        in_specs=[whole(), whole()],
        out_specs=(whole(), whole()),
        compiler_params=params(),
        name="finish",
    )(gram, sketch)


def solution(mesh):
    placed = (P("space", None), P("space", None), P("probe", None), P())
    return jax.shard_map(
        on_device,
        mesh=mesh,
        in_specs=placed,
        out_specs=(P(None, ("space", "probe")), P()),
        check_vma=False,
    )
```

time: 571 us -> 90.6 us (0.16)
  other arithmetic: 172 us -> 1.72 us
  blocking collectives: 159 us -> 0 us
  local copies, waits for them, and re-layouts: 117 us -> 1.17 us
  starting transfers between devices: 115 us -> 0 us
  Pallas kernels: 0 us -> 84 us
    add x32 -> x1, other arithmetic: 136 us -> 0.02 us  [body(): turn * GROUP + slot_probe[:, None]]
    ppermute x34 -> x0, starting transfers between devices: 115 us -> none  [the longest x17 93.6 us: padded_2(): lax.ppermute(tail, axis, [(i, (i + 1) % count) for i in range(ends)])]
    psum x1 -> x0, blocking collectives: 115 us -> none  [on_device(): gram = lax.psum(gram_part, ('space', 'probe'))]
    pallas_call x0 -> x7, Pallas kernels: none -> 84 us  [the longest x1 23.5 us: on_device(): pl.pallas_call(sum_kernel, out_shape=jax.ShapeDtypeStruct((GROUP, 4, 128)...]
    slice x50 -> x0, local copies, waits for them, and re-layouts: 45.6 us -> none  [the longest x16 26.4 us: apply_operator(): below_y = jnp.concatenate([zeros_y, centre[..., :-layer]], -1)]
    all_to_all x1 -> x0, blocking collectives: 43.9 us -> none  [on_device(): lax.all_to_all(flat_fields, 'probe', split_axis=1, concat_axis=0, tiled=T...]
    dynamic_slice x16 -> x0, local copies, waits for them, and re-layouts: 22.8 us -> none  [single(): search = table[step, 0] * search + table[step, 1] * resid]
    while x16 -> x1, local copies, waits for them, and re-layouts: 19.6 us -> 0.07 us
  transfers between devices with their start and end apart: 34 -> 0, of which waited for: 0 -> 0; matrix products, arithmetic and copies ran while one was open for 24% -> 0% of each run, Pallas kernels for 0% -> 0%
where the time goes in v1:
time: 90.6 us; the launch traced here: 90.3 us
  Pallas kernels  84 us (93%)
  between operations  3.29 us (4%)
  other arithmetic  1.72 us (2%)
  local copies, waits for them, and re-layouts  1.17 us (1%)
    pallas_call x1, Pallas kernels, on_device(): pl.pallas_call(sum_kernel, out_shape=jax.ShapeDtypeStruct((GROUP, 4, 128)...  23.5 us
    pallas_call x1, Pallas kernels, body(): pl.pallas_call(window_kernel, out_shape=(jax.ShapeDtypeStruct((SPAN, 2, Q...  22.1 us
    pallas_call x1, Pallas kernels, body(): pl.pallas_call(spread_kernel, out_shape=jax.ShapeDtypeStruct((2, CHIPS, S...  16.2 us
    pallas_call x1, Pallas kernels, on_device(): pl.pallas_call(finish_kernel, out_shape=(jax.ShapeDtypeStruct((probes, ce...  10.7 us
    pallas_call x1, Pallas kernels, body(): pl.pallas_call(place_kernel, out_shape=(jax.ShapeDtypeStruct(sketch.shape...  7.42 us
    pallas_call x1, Pallas kernels, body(): pl.pallas_call(solve_kernel, out_shape=jax.ShapeDtypeStruct((SPAN, 8, QUA...  3.1 us

profile of v1, /device:TPU:1, one launch (start us, length us, event | category | flops | bytes accessed | tf_op | source)
XLA Modules:
  0.0 90.3 jit_solution(4171391777673979680)
XLA Ops:
  0.6 0.7 and_select_fusion.4
  1.3 0.2 convert_reduce_fusion
  1.5 0.6 reduce_max.27
  4.8 0.0 copy-start
  4.8 0.0 copy-start.1
  4.8 0.1 broadcast_in_dim.37
  4.9 0.0 copy-start.2
  4.9 0.0 copy-start.3
  4.9 0.6 broadcast_in_dim.38
  5.5 0.2 copy-done
  5.7 0.1 copy-done.1
  5.8 0.0 copy-done.2
  5.8 0.0 copy-done.3
  5.8 50.2 %while.13 = (s32[]{:T(128)}, f32[64,4096]{1,0:T(8,128)S(1)}, f32[16,4,128]{2,1,0:T(4,128)}, s32[]{:T(128)}, s32[256]{0:T(256)S(1)}, /*index=5*/s32[256]{0:T(256)...) while((s32[]{:T(128)}, f32[64,4096]{1,0:T(8,128)S(1)}, ...), condition=%wide.region_5.6_spmd.clone, body=%wide.region_2.5_spmd.clone.sunk | while | flops 145683 | bytes 2103761 | solution.py:508
  5.8 0.2 fusion.15
  6.0 0.1 reshape.28.cell_ref
  6.1 1.0 %cut.1.own_ref = f32[5,2,8,8,128]{4,3,2,1,0:T(8,128)S(1)} custom-call(s32[2,40]{1,0:T(2,128)S(1)} %reshape.28.cell_ref, f32[8,8192]{1,0:T(8,128)S(1)} %get-tuple-element.248.cond_ref, f32[8,8192]{1,0:T(8,128)S(1)} %get-tuple-element.249.leak_ref), custom_call_target="tpu_custom_call" | custom-call | tf_op jit(solution)/shard_map/while/body/cut/pallas_call | solution.py:449
  7.1 22.1 %windows.1 = (f32[5,2,8,8,128]{4,3,2,1,0:T(8,128)S(1)}, s32[2,8,4,256]{3,2,1,0:T(4,128)S(1)}) custom-call(f32[5,2,8,8,128]{4,3,2,1,0:T(8,128)S(1)} %cut.1.own_ref, s32[4,256]{1,0:T(4,128)S(1)} %get-tuple-element.250.signs_ref), custom_call_target="tpu_custom_call" | custom-call | tf_op jit(solution)/shard_map/while/body/windows/pallas_call | solution.py:457
  29.2 3.1 %solve.1.own_ref = f32[5,8,8,128]{3,2,1,0:T(8,128)S(1)} custom-call(s32[2,40]{1,0:T(2,128)S(1)} %reshape.28.cell_ref, f32[5,2,8,8,128]{4,3,2,1,0:T(8,128)S(1)} %get-tuple-element.210.win_ref), custom_call_target="tpu_custom_call" | custom-call | tf_op jit(solution)/shard_map/while/body/solve/pallas_call | solution.py:469
  32.3 16.2 %spread.1 = f32[2,8,5,8,128]{4,3,2,1,0:T(8,128)S(1)} custom-call(f32[5,8,8,128]{3,2,1,0:T(8,128)S(1)} %solve.1.own_ref), custom_call_target="tpu_custom_call" | custom-call | tf_op jit(solution)/shard_map/while/body/spread/pallas_call | solution.py:483
  48.6 0.1 copy.18.before_ref
  48.6 7.4 %place.1 = (f32[64,4096]{1,0:T(8,128)S(1)}, f32[16,4,128]{2,1,0:T(4,128)}) custom-call(s32[1]{0:T(128)} %bitcast.8.turn_ref, s32[2,40]{1,0:T(2,128)S(1)} %reshape.28.cell_ref, f32[2,40,8,128]{3,2,1,0:T(8,128)S(1)} %bitcast.10, s32[1,128]{1,0:T(1,128)S(1)} %pad_bitcast_fusion.2.slot_ref, s32[2,8,4,256]{3,2,1,0:T(4,128)S(1)} %get-tuple-element.212.signs_ref, ...), custom_call_target="tpu_custom_call" | custom-call | tf_op jit(solution)/shard_map/while/body/place/pallas_call | solution.py:492
  56.1 23.5 %gram_sum.1.gram_ref = f32[16,4,128]{2,1,0:T(4,128)S(1)} custom-call(f32[16,4,128]{2,1,0:T(4,128)} %get-tuple-element.74.part_ref), custom_call_target="tpu_custom_call" | custom-call | tf_op jit(solution)/shard_map/gram_sum/pallas_call | solution.py:509
  79.6 10.7 %finish.1 = (f32[64,4096]{1,0:T(8,128)}, f32[64,64]{1,0:T(8,128)}) custom-call(f32[16,4,128]{2,1,0:T(4,128)S(1)} %gram_sum.1.gram_ref, f32[64,4096]{1,0:T(8,128)S(1)} %get-tuple-element.75.sketch_ref), custom_call_target="tpu_custom_call" | custom-call | tf_op jit(solution)/shard_map/finish/pallas_call | solution.py:530
  (2 shorter events, 0.0 us)
Async XLA Ops:
  4.8 1.0 %copy-start = (f32[8,8192]{1,0:T(8,128)S(1)}, f32[8,8192]{1,0:T(8,128)}, u32[]{:S(2)}) copy-start(f32[8,8192]{1,0:T(8,128)} %param.6) | copy-start | bytes 786436
  4.8 1.0 %copy-start.1 = (f32[8,8192]{1,0:T(8,128)S(1)}, f32[8,8192]{1,0:T(8,128)}, u32[]{:S(2)}) copy-start(f32[8,8192]{1,0:T(8,128)} %param.7) | copy-start | bytes 786436
  4.9 0.9 %copy-start.2 = (s32[4,256]{1,0:T(4,128)S(1)}, s32[4,256]{1,0:T(4,128)}, u32[]{:S(2)}) copy-start(s32[4,256]{1,0:T(4,128)} %param.8) | copy-start | bytes 12292
  4.9 0.9 %copy-start.3 = (s32[256]{0:T(256)S(1)}, s32[256]{0:T(256)}, u32[]{:S(2)}) copy-start(s32[256]{0:T(256)} %param.9) | copy-start | bytes 3076

commit v2 on v0

v2 whole, which is shorter than its diff:
```python
import functools
import math

import jax
import jax.numpy as jnp
from jax import lax
from jax.experimental import pallas as pl
from jax.experimental.pallas import tpu as pltpu
from jax.sharding import PartitionSpec as P

NZ = 64
SWEEPS = 16
REACH = 2
SPAN = 2 * REACH + 1
GROUP = 16
CHIPS = 8
SLOTS = GROUP * SPAN
QUADS = 8
PAIRS = 32

bound_low = 0.005
bound_high = 24.5

F32 = jnp.float32
VMEM = pltpu.VMEM
SMEM = pltpu.SMEM


def chebyshev_table(count):
    center = 0.5 * (bound_high + bound_low)
    spread = 0.5 * (bound_high - bound_low)
    ratio = center / spread
    rho_prev = 1.0 / ratio
    entries = []
    for index_step in range(count):
        rho_next = 1.0 / (2.0 * ratio - rho_prev)
        entries.append((rho_next * rho_prev, 2.0 * rho_next / spread))
        rho_prev = rho_next
    return entries


def start_scale():
    return 1.0 / (0.5 * (bound_high + bound_low))


def decode(cell):
    cell = jnp.maximum(cell, 0)
    x = lax.shift_right_logical(cell, 13)
    y = lax.bitwise_and(lax.shift_right_logical(cell, 6), 127)
    z = lax.bitwise_and(cell, 63)
    y_first = lax.bitwise_and(y + 1, 126 + 128) - 16
    return x, y, y_first, z, z - 15


def lanes(shape=(8, 128)):
    return lax.broadcasted_iota(jnp.int32, shape, 1)


def sublanes(shape=(8, 128)):
    return lax.broadcasted_iota(jnp.int32, shape, 0)


def wrap(shift):
    return lax.bitwise_and(shift, 127)


OFFSETS = (-2, 2, -1, 1)


def barrier_with(partners):
    barrier = pltpu.get_barrier_semaphore()
    for partner in partners:
        pl.semaphore_signal(barrier, inc=1, device_id=partner, device_id_type=pl.DeviceIdType.MESH)
    return lambda: pl.semaphore_wait(barrier, len(partners))


def remote(src, dst, send, recv, device):
    return pltpu.make_async_remote_copy(
        src_ref=src, dst_ref=dst, send_sem=send, recv_sem=recv, device_id=device, device_id_type=pl.DeviceIdType.MESH
    )


def cut_kernel(cells_ref, cond_ref, leak_ref, out_ref):
    me = lax.axis_index("probe")
    lane = lanes()
    for e in range(SPAN):
        _, _, y_first, _, z_first = decode(cells_ref[me % 2 * (SLOTS // 2) + me // 2 * SPAN + e])
        pair_first = y_first // 2
        shifts = [wrap(128 - z_first), wrap(96 - z_first), wrap(192 - z_first), wrap(160 - z_first)]
        for k in range(QUADS):
            one = pl.multiple_of(jnp.clip(pair_first + 2 * k, 0, 63) * 128, 128)
            two = pl.multiple_of(jnp.clip(pair_first + 2 * k + 1, 0, 63) * 128, 128)
            for prop, ref in enumerate((cond_ref, leak_ref)):
                a = ref[:, pl.ds(one, 128)]
                b = ref[:, pl.ds(two, 128)]
                low = jnp.where(lane < 32, pltpu.roll(a, shifts[0], 1), pltpu.roll(a, shifts[1], 1))
                high = jnp.where(lane < 96, pltpu.roll(b, shifts[2], 1), pltpu.roll(b, shifts[3], 1))
                out_ref[e, prop, k] = jnp.where(lane < 64, low, high)


def faces(cell, here, win_ref, coef):
    _, _, y_first, _, z_first = decode(cell)
    lane = lanes()
    sub = sublanes()
    group = lane // 32
    zz = z_first + lane % 32
    z_ok = (zz >= 0) & (zz < NZ)
    for b in range(SPAN):
        xx = (here + (b - REACH)) * 8 + sub
        x_ok = (xx >= 0) & (xx < 256)
        for k in range(QUADS):
            yy = y_first + 4 * k + group
            inside = x_ok & (yy >= 0) & (yy < 128) & z_ok
            own = win_ref[b, 0, k]
            before = win_ref[max(b - 1, 0), 0, k]
            after = win_ref[min(b + 1, SPAN - 1), 0, k]
            left = win_ref[b, 0, max(k - 1, 0)]
            right = win_ref[b, 0, min(k + 1, QUADS - 1)]
            parts = (
                (jnp.where(sub == 0, pltpu.roll(before, 1, 0), pltpu.roll(own, 1, 0)), xx >= 1),
                (jnp.where(sub == 7, pltpu.roll(after, 7, 0), pltpu.roll(own, 7, 0)), xx < 255),
                (jnp.where(group == 0, pltpu.roll(left, 32, 1), pltpu.roll(own, 32, 1)), yy >= 1),
                (jnp.where(group == 3, pltpu.roll(right, 96, 1), pltpu.roll(own, 96, 1)), yy < 127),
                (pltpu.roll(own, 1, 1), zz >= 1),
                (pltpu.roll(own, 127, 1), zz < NZ - 1),
            )
            diagonal = win_ref[b, 1, k]
            for n, (other, there) in enumerate(parts):
                face = 0.5 * (own + jnp.where(there, other, own))
                diagonal = diagonal + face
                coef[n + 1, b, k] = jnp.where(inside & there, face, 0.0)
            coef[0, b, k] = diagonal


def start_fields(cell, here, search, resid, total):
    x, y, y_first, _, _ = decode(cell)
    lane = lanes()
    sub = sublanes()
    weight = jnp.where(cell >= 0, 1.0, 0.0).astype(F32)
    zero = jnp.zeros((8, 128), F32)
    for b in range(SPAN):
        for k in range(QUADS):
            search[1, b, k] = zero
            if b == REACH and k in (3, 4):
                hit = (sub == x - here * 8) & (4 * k + lane // 32 == y - y_first) & (lane % 32 == 15)
                source = jnp.where(hit, weight, 0.0)
                resid[b, k] = source
                search[0, b, k] = source * start_scale()
            else:
                resid[b, k] = zero
                search[0, b, k] = zero
            total[b, k] = zero


def sweeps(coef, search, resid, total):
    group = lanes() // 32
    sub = sublanes()
    zero = jnp.zeros((8, 128), F32)
    table = chebyshev_table(SWEEPS)
    for j in range(SWEEPS - 1):
        a, c = (float(value) for value in table[j])
        now, later = j % 2, (j + 1) % 2
        wide = j + 1
        k_low, k_high = (15 - wide) // 4, (16 + wide) // 4
        b_low, b_high = (1, 3) if wide <= 8 else (0, 4)
        for b in range(b_low, b_high + 1):
            for k in range(k_low, k_high + 1):
                own = search[now, b, k]
                edge = pltpu.roll(search[now, b - 1, k], 1, 0) if b > 0 else zero
                down = jnp.where(sub == 0, edge, pltpu.roll(own, 1, 0))
                edge = pltpu.roll(search[now, b + 1, k], 7, 0) if b < SPAN - 1 else zero
                up = jnp.where(sub == 7, edge, pltpu.roll(own, 7, 0))
                edge = pltpu.roll(search[now, b, k - 1], 32, 1) if k > 0 else zero
                left = jnp.where(group == 0, edge, pltpu.roll(own, 32, 1))
                edge = pltpu.roll(search[now, b, k + 1], 96, 1) if k < QUADS - 1 else zero
                right = jnp.where(group == 3, edge, pltpu.roll(own, 96, 1))
                image = coef[0, b, k] * own
                image = image - coef[1, b, k] * down
                image = image - coef[2, b, k] * up
                image = image - coef[3, b, k] * left
                image = image - coef[4, b, k] * right
                image = image - coef[5, b, k] * pltpu.roll(own, 1, 1)
                image = image - coef[6, b, k] * pltpu.roll(own, 127, 1)
                rest = resid[b, k] - image
                resid[b, k] = rest
                total[b, k] = total[b, k] + own
                search[later, b, k] = a * own + c * rest


def split2(value):
    high = value.astype(jnp.bfloat16)
    return high, (value - high.astype(F32)).astype(jnp.bfloat16)


def moves(cell):
    shape = (256, 128)
    _, _, y_first, _, z_first = decode(jnp.broadcast_to(cell[0:1, :], shape))
    lane = lanes(shape)
    row = sublanes(shape)
    odd = lax.bitwise_and(lax.shift_right_arithmetic(y_first, 1), 1)
    same_z = lax.bitwise_and(row + z_first, 31) == lax.bitwise_and(lane, 31)
    same_y = lax.bitwise_and(lax.shift_right_logical(row, 5) + 2 * odd, 3) == lax.shift_right_logical(lane, 5)
    hit = same_z & same_y & ((row < 128) == (lane < 64))
    return jnp.where(hit, 1.0, 0.0).astype(jnp.bfloat16)


def align(first, second, b, move, total, out_ref):
    one = split2(jnp.concatenate([total[b, lax.bitwise_and(k - first, 7)] for k in range(QUADS)], axis=0))
    two = split2(jnp.concatenate([total[b, lax.bitwise_and(k - second, 7)] for k in range(QUADS)], axis=0))
    both = jnp.concatenate([jnp.concatenate(part, axis=1) for part in zip(one, two)], axis=0)
    both = jnp.dot(both, move[...], preferred_element_type=F32)
    both = both[:64] + both[64:]
    for k in range(QUADS):
        out_ref[b, :, k, :] = both[8 * k : 8 * k + 8]


def panel(signs, slot_ref, cell_lane, cell_down, half, keep, before_ref, rows_ref, out_ref):
    table = jnp.concatenate([signs[p % 2, p // 2] for p in range(GROUP)], axis=0)
    table = (2 * table - 1).astype(jnp.bfloat16)
    which = lax.broadcasted_iota(jnp.int32, (256, 128), 0) == slot_ref[...]
    pick = jnp.dot(table, which.astype(F32).astype(jnp.bfloat16), preferred_element_type=F32)
    _, _, y_first, _, _ = decode(cell_lane[...])
    pair_first = lax.shift_right_arithmetic(y_first, 1) - PAIRS * half
    _, _, _, _, z_first = decode(cell_down[...])
    lane = lanes((SLOTS, 128))
    z_here = lane % 64 - z_first
    shown = (z_here >= 0) & (z_here < 32)
    group = lane // 32
    blank = jnp.zeros((128 - SLOTS, 128), jnp.bfloat16)
    for k in range(QUADS):
        own = rows_ref[pl.ds(k, SLOTS, stride=8), :]
        r1, r2, r3 = (pltpu.roll(own, 32 * n, 1) for n in (1, 2, 3))
        pairs = (
            jnp.where(group == 0, own, jnp.where(group == 3, r2, r1)),
            jnp.where(group == 0, r2, jnp.where(group == 3, own, r3)),
        )
        for m in range(2):
            high, low = split2(jnp.where(shown, pairs[m], 0.0))
            value = jnp.concatenate([high, blank, low, blank], axis=0)
            left = []
            for t in (2 * k + m, 2 * k + m + 16):
                ok = (pair_first <= t) & (t < pair_first + 16)
                left.append(jnp.where(ok, pick, 0.0).astype(jnp.bfloat16))
            left = jnp.concatenate(left, axis=0)
            both = jnp.dot(jnp.concatenate([left, left], axis=1), value, preferred_element_type=F32)
            for n in range(2):
                at = 128 * (2 * k + m + 16 * n)
                part = both[64 * n : 64 * n + 64]
                out_ref[:, at : at + 128] = part + keep * before_ref[:, at : at + 128]


def gram_of(sketch_ref):
    both = jnp.concatenate(split2(sketch_ref[...]), axis=0)
    full = lax.dot_general(both, both, (((1,), (1,)), ((), ())), preferred_element_type=F32)
    return full[:64, :64] + ((full[:64, 64:] + full[64:, :64]) + full[64:, 64:])


def sketch_kernel(
    own_scalar,
    own_cell,
    keep_ref,
    cuts,
    signs_ref,
    slot_ref,
    cell_lane,
    cell_down,
    before_ref,
    sketch_ref,
    gram_ref,
    win,
    signs,
    coef,
    search,
    resid,
    total,
    fields,
    block,
    rows,
    move,
    mine,
    twin_buf,
    y_buf,
    z_buf,
    x_buf,
    win_sem,
    sign_sem,
    sign_pair,
    near_sem,
    row_sem,
    pair_sem,
    twin_sem,
    y_sem,
    z_sem,
    x_sem,
    last_sem,
):
    count = lax.axis_size("space")
    here = lax.axis_index("space")
    me = lax.axis_index("probe")
    chip = me // 2
    core = me % 2
    x = here // 8
    z = here % 8
    near = [(lax.rem(here + d + count, count), me) for d in OFFSETS]
    along = [(here, lax.rem(chip + r, CHIPS) * 2 + core) for r in range(1, CHIPS)]
    ring_z = [(x * 8 + lax.rem(z + r, 8), me) for r in range(1, 8)]
    ring_x = [(lax.rem(x + r, 4) * 8 + z, me) for r in range(1, 4)]
    twin = (here, chip * 2 + 1 - core)
    entered = barrier_with(near + along + [twin] + ring_z + ring_x)
    cell = own_cell[...]
    start_fields(cell, here, search, resid, total)
    move[...] = moves(cell)
    entered()
    sent = []
    windows = []
    for i, d in enumerate(OFFSETS):
        copy = remote(cuts.at[d + 2], win.at[2 - d], win_sem.at[0, i], win_sem.at[1, i], near[i])
        copy.start()
        windows.append(copy)
    shared = []
    for r in range(1, CHIPS):
        copy = remote(signs_ref, signs.at[core, chip], sign_sem.at[0, r], sign_sem.at[1, r], along[r - 1])
        copy.start()
        shared.append(copy)
    win[REACH] = cuts[REACH]
    signs[core, chip] = signs_ref[...]
    for copy in windows:
        copy.wait_recv()
    faces(cell, here, win, coef)
    sweeps(coef, search, resid, total)
    spread = []
    last = (SWEEPS - 1) % 2
    for b in range(SPAN):
        for k in range(QUADS):
            total[b, k] = total[b, k] + search[last, b, k]
    _, _, y_first, _, _ = decode(own_scalar[0])
    second = lax.shift_right_arithmetic(y_first, 2)
    first = second + lax.bitwise_and(lax.shift_right_arithmetic(y_first, 1), 1)
    for i, d in enumerate(OFFSETS):
        align(first, second, d + 2, move, total, fields)
        copy = remote(
            fields.at[d + 2], block.at[:, pl.ds(8 * (2 - d), 8)], near_sem.at[0, i], near_sem.at[1, i], near[i]
        )
        copy.start()
        spread.append(copy)
    align(first, second, REACH, move, total, fields)
    block[:, 8 * REACH : 8 * REACH + 8] = fields[REACH]
    for copy in shared:
        copy.wait_recv()
    pair = remote(signs.at[core], signs.at[core], sign_pair.at[0], sign_pair.at[1], twin)
    pair.start()
    sent += windows + shared + spread + [pair]
    for copy in spread:
        copy.wait_recv()
    out = []
    place = pl.ds(pl.multiple_of((core * CHIPS + chip) * 8 * SPAN, 8), 8 * SPAN)
    for r in range(1, CHIPS):
        target = lax.rem(chip + r, CHIPS)
        copy = remote(block.at[target], rows.at[place], row_sem.at[0, r], row_sem.at[1, r], along[r - 1])
        copy.start()
        out.append(copy)
    rows[place, :] = block[chip]
    pairs = []
    for r in (0, 1, 7, 2, 6, 3, 5, 4):
        source = lax.rem(chip - r + CHIPS, CHIPS)
        if r:
            out[r - 1].wait_recv()
        part = rows.at[pl.ds(pl.multiple_of((core * CHIPS + source) * 8 * SPAN, 8), 8 * SPAN)]
        copy = remote(part, part, pair_sem.at[0, r], pair_sem.at[1, r], twin)
        copy.start()
        pairs.append(copy)
    pair.wait_recv()
    for copy in pairs:
        copy.wait_recv()
    sent += out + pairs
    panel(signs, slot_ref, cell_lane, cell_down, core, keep_ref[...], before_ref, rows, sketch_ref)
    gram = gram_of(sketch_ref)
    for h in range(2):
        mine[h] = jnp.concatenate([gram[32 * h : 32 * h + 16], gram[32 * h + 16 : 32 * h + 32]], axis=1)
    copy = remote(mine.at[1 - core], twin_buf, twin_sem.at[0], twin_sem.at[1], twin)
    copy.start()
    sent.append(copy)
    copy.wait_recv()
    value = mine[core] + twin_buf[...]
    for buf, sem, at, ring in ((y_buf, y_sem, chip, along), (z_buf, z_sem, z, ring_z), (x_buf, x_sem, x, ring_x)):
        buf[at] = value
        steps = []
        for r, device in enumerate(ring):
            copy = remote(buf.at[at], buf.at[at], sem.at[0, r], sem.at[1, r], device)
            copy.start()
            steps.append(copy)
        for copy in steps:
            copy.wait_recv()
        sent += steps
        value = buf[0]
        for r in range(1, len(ring) + 1):
            value = value + buf[r]
    gram_ref[core] = value
    copy = remote(gram_ref.at[core], gram_ref.at[core], last_sem.at[0], last_sem.at[1], twin)
    copy.start()
    copy.wait_recv()
    for item in sent + [copy]:
        item.wait_send()


def finish_kernel(gram_ref, sketch_ref, basis_ref, factor_ref):
    shape = (8, 128)
    lane = lanes(shape)
    sub = sublanes(shape)
    rows = []
    for i in range(8):
        block = gram_ref[i // 4, 8 * (i % 2) : 8 * (i % 2) + 8, :]
        if i % 4 >= 2:
            block = pltpu.roll(block, 64, 1)
        rows.append(jnp.where(lane < 64, block, jnp.where(lane - 64 == sub + 8 * i, 1.0, 0.0)))
    for n in range(8):
        columns = [[jnp.broadcast_to(rows[i][:, 8 * n + c : 8 * n + c + 1], shape) for i in range(n, 8)] for c in range(8)]
        own = rows[n]
        lines = []
        for c in range(8):
            pivot = jnp.broadcast_to(columns[c][0][c : c + 1, :], shape)
            scale = lax.rsqrt(pivot)
            scale = scale * (1.5 - 0.5 * pivot * scale * scale)
            line = jnp.broadcast_to(own[c : c + 1, :], shape) * scale
            columns[c] = [value * scale for value in columns[c]]
            below = jnp.where(sub > c, columns[c][0], 0.0)
            own = jnp.where(sub == c, line, own - below * line)
            for later in range(c + 1, 8):
                factor = jnp.broadcast_to(columns[c][0][later : later + 1, :], shape)
                columns[later][0] = columns[later][0] - below * factor
                for i in range(1, 8 - n):
                    columns[later][i] = columns[later][i] - columns[c][i] * factor
            lines.append(line)
        rows[n] = own
        for i in range(n + 1, 8):
            value = rows[i]
            for c in range(8):
                value = value - columns[c][i - n] * lines[c]
            rows[i] = value
    full = jnp.concatenate(rows, axis=0)
    row_at = lax.broadcasted_iota(jnp.int32, (64, 64), 0)
    col_at = lax.broadcasted_iota(jnp.int32, (64, 64), 1)
    upper = jnp.where(col_at >= row_at, full[:, :64], 0.0)
    factor_ref[...] = upper * (1.0 / math.sqrt(256))
    high, low = split2(full[:, 64:] * math.sqrt(256 * 128 * 64))
    left = jnp.concatenate([high, high, low], axis=1)
    for t in range(8):
        high, low = split2(sketch_ref[:, 512 * t : 512 * t + 512])
        right = jnp.concatenate([high, low, high], axis=0)
        basis_ref[:, 512 * t : 512 * t + 512] = jnp.dot(left, right, preferred_element_type=F32)


def params(**more):
    return pltpu.CompilerParams(vmem_limit_bytes=48 * 1024 * 1024, **more)


def whole(space=VMEM):
    return pl.BlockSpec(memory_space=space)


def dma(*shape):
    return pltpu.SemaphoreType.DMA(shape)


def on_device(conductivity, leakage, signs, wells):
    here = lax.axis_index("space")
    chip = lax.axis_index("probe") // 2
    core = lax.axis_index("probe") % 2
    cells = conductivity.shape[0] * conductivity.shape[1]
    probes = signs.shape[0] * GROUP
    count = wells.shape[0]
    owner = wells // cells
    index = jnp.arange(count, dtype=jnp.int32)
    rank = jnp.sum((owner[None, :] == owner[:, None]) & (index[None, :] < index[:, None]), axis=1, dtype=jnp.int32)
    rounds = jnp.max(rank) // GROUP + 1
    slot = jnp.arange(128, dtype=jnp.int32)
    slot_probe = jnp.where(slot < SLOTS, (slot % (SLOTS // 2)) // SPAN * 2 + slot // (SLOTS // 2), count)
    slot_block = here + slot % SPAN - REACH

    def body(carry):
        turn, sketch, _ = carry
        match = (owner[None, :] == slot_block[:, None]) & (rank[None, :] - turn * GROUP == slot_probe[:, None])
        chosen = jnp.max(jnp.where(match, index[None, :], -1), axis=1)
        cell = jnp.max(jnp.where(match, wells[None, :], -1), axis=1)
        cuts = pl.pallas_call(
            cut_kernel,
            out_shape=jax.ShapeDtypeStruct((SPAN, 2, QUADS, 8, 128), F32),
            in_specs=[whole(SMEM), whole(), whole()],
            out_specs=whole(),
            compiler_params=params(),
            name="cut",
        )(cell, conductivity, leakage)
        own = cell[core * (SLOTS // 2) + chip * SPAN + REACH]
        field = VMEM((SPAN, QUADS, 8, 128), F32)
        sketch, gram = pl.pallas_call(
            sketch_kernel,
            out_shape=(
                jax.ShapeDtypeStruct(sketch.shape, F32),
                jax.ShapeDtypeStruct((2, 16, 128), F32),
            ),
            in_specs=[whole(SMEM)] + [whole()] * 8,
            out_specs=(whole(), whole()),
            scratch_shapes=[
                VMEM((SPAN, 2, QUADS, 8, 128), F32),
                VMEM((2, CHIPS, probes // GROUP, count), jnp.int32),
                VMEM((7, SPAN, QUADS, 8, 128), F32),
                VMEM((2, SPAN, QUADS, 8, 128), F32),
                field,
                field,
                VMEM((SPAN, 8, QUADS, 128), F32),
                VMEM((8, SPAN * QUADS, 128), F32),
                VMEM((SLOTS * QUADS, 128), F32),
                VMEM((256, 128), jnp.bfloat16),
                VMEM((2, 16, 128), F32),
                VMEM((16, 128), F32),
                VMEM((8, 16, 128), F32),
                VMEM((8, 16, 128), F32),
                VMEM((4, 16, 128), F32),
                dma(2, 4),
                dma(2, 8),
                dma(2),
                dma(2, 4),
                dma(2, 8),
                dma(2, 8),
                dma(2),
                dma(2, 8),
                dma(2, 8),
                dma(2, 4),
                dma(2),
            ],
            compiler_params=params(collective_id=0, has_side_effects=True),
            name="sketch",
        )(
            own.reshape(1),
            jnp.broadcast_to(own, (8, 128)),
            jnp.broadcast_to((turn > 0).astype(F32), (1, 128)),
            cuts,
            signs,
            chosen[None, :],
            cell[None, :],
            jnp.broadcast_to(cell[:SLOTS, None], (SLOTS, 128)),
            sketch,
        )
        return turn + 1, sketch, gram

    sketch = jnp.zeros((probes, cells // GROUP), F32)
    gram = jnp.zeros((2, 16, 128), F32)
    _, sketch, gram = lax.while_loop(lambda carry: carry[0] < rounds, body, (jnp.int32(0), sketch, gram))
    return pl.pallas_call(
        finish_kernel,
        out_shape=(
            jax.ShapeDtypeStruct((probes, cells // GROUP), F32),
            jax.ShapeDtypeStruct((probes, probes), F32),
        ),
        in_specs=[whole(), whole()],
        out_specs=(whole(), whole()),
        compiler_params=params(),
        name="finish",
    )(gram, sketch)


def solution(mesh):
    placed = (P("space", None), P("space", None), P("probe", None), P())
    return jax.shard_map(
        on_device,
        mesh=mesh,
        in_specs=placed,
        out_specs=(P(None, ("space", "probe")), P()),
        check_vma=False,
    )
```

time: 571 us -> 70.1 us (0.12)
  other arithmetic: 172 us -> 1.05 us
  blocking collectives: 159 us -> 0 us
  starting transfers between devices: 115 us -> 0 us
  local copies, waits for them, and re-layouts: 117 us -> 3.72 us
  Pallas kernels: 0 us -> 61.7 us
    add x32 -> x0, other arithmetic: 136 us -> none  [the longest x16 100 us: single(): search = table[step, 0] * search + table[step, 1] * resid]
    ppermute x34 -> x0, starting transfers between devices: 115 us -> none  [the longest x17 93.6 us: padded_2(): lax.ppermute(tail, axis, [(i, (i + 1) % count) for i in range(ends)])]
    psum x1 -> x0, blocking collectives: 115 us -> none  [on_device(): gram = lax.psum(gram_part, ('space', 'probe'))]
    pallas_call x0 -> x3, Pallas kernels: none -> 61.7 us  [the longest x1 56.5 us: body(): pl.pallas_call(sketch_kernel, out_shape=(jax.ShapeDtypeStruct(sketch.shap...]
    slice x50 -> x0, local copies, waits for them, and re-layouts: 45.6 us -> none  [the longest x16 26.4 us: apply_operator(): below_y = jnp.concatenate([zeros_y, centre[..., :-layer]], -1)]
    all_to_all x1 -> x0, blocking collectives: 43.9 us -> none  [on_device(): lax.all_to_all(flat_fields, 'probe', split_axis=1, concat_axis=0, tiled=T...]
    dynamic_slice x16 -> x1, local copies, waits for them, and re-layouts: 22.8 us -> 0.65 us  [body(): own = cell[core * (SLOTS // 2) + chip * SPAN + REACH]]
    while x16 -> x1, local copies, waits for them, and re-layouts: 19.6 us -> 0.07 us
  transfers between devices with their start and end apart: 34 -> 0, of which waited for: 0 -> 0; matrix products, arithmetic and copies ran while one was open for 24% -> 0% of each run, Pallas kernels for 0% -> 0%
where the time goes in v2:
time: 70.1 us; the launch traced here: 69.8 us
  Pallas kernels  61.7 us (88%)
  local copies, waits for them, and re-layouts  3.72 us (5%)
  between operations  3.29 us (5%)
  other arithmetic  1.05 us (1%)
    pallas_call x1, Pallas kernels, body(): pl.pallas_call(sketch_kernel, out_shape=(jax.ShapeDtypeStruct(sketch.shap...  56.5 us
    pallas_call x1, Pallas kernels, on_device(): pl.pallas_call(finish_kernel, out_shape=(jax.ShapeDtypeStruct((probes, ce...  4.27 us
    unnamed x8, local copies, waits for them, and re-layouts  1.63 us

profile of v2, /device:TPU:1, one launch (start us, length us, event | category | flops | bytes accessed | tf_op | source)
XLA Modules:
  0.0 69.8 jit_solution(16718420330450412567)
XLA Ops:
  0.7 0.0 copy-start.3
  0.7 0.7 copy-done.3
  1.3 0.2 convert_reduce_fusion
  1.5 0.6 reduce_max.29
  4.8 0.6 broadcast_in_dim.63
  5.4 0.0 copy-start
  5.4 0.0 copy-start.1
  5.4 0.0 copy-start.2
  5.4 0.1 broadcast_in_dim.62
  5.4 0.9 %copy-done = f32[8,8192]{1,0:T(8,128)S(1)} copy-done((f32[8,8192]{1,0:T(8,128)S(1)}, f32[8,8192]{1,0:T(8,128)}, u32[]{:S(2)}) %copy-start) | copy-done | bytes 262168
  6.3 0.1 copy-done.1
  6.4 0.0 copy-done.2
  6.4 59.2 %while.15 = (s32[]{:T(128)}, f32[64,4096]{1,0:T(8,128)S(1)}, f32[2,16,128]{2,1,0:T(8,128)}, s32[]{:T(128)}, s32[256]{0:T(256)S(1)}, /*index=5*/s32[256]{0:T(256)...) while((s32[]{:T(128)}, f32[64,4096]{1,0:T(8,128)S(1)}, ...), condition=%wide.region_5.6_spmd.clone, body=%wide.region_2.5_spmd.clone.sunk | while | flops 233477 | bytes 2151435 | solution.py:548
  6.4 0.1 copy.16.before_ref
  6.5 0.2 fusion.12
  6.7 0.7 dynamic_slice.5.own_scalar
  7.4 0.6 broadcast_in_dim.88.own_cell
  8.0 0.1 broadcast_in_dim.90.cell_down
  8.1 1.0 %cut.1.cuts = f32[5,2,8,8,128]{4,3,2,1,0:T(8,128)S(1)} custom-call(s32[128]{0:T(128)S(1)} %get-tuple-element.319.cells_ref, f32[8,8192]{1,0:T(8,128)S(1)} %get-tuple-element.361.cond_ref, f32[8,8192]{1,0:T(8,128)S(1)} %get-tuple-element.362.leak_ref), custom_call_target="tpu_custom_call" | custom-call | tf_op jit(solution)/shard_map/while/body/cut/pallas_call | solution.py:485
  9.1 56.5 %sketch.3 = (f32[64,4096]{1,0:T(8,128)S(1)}, f32[2,16,128]{2,1,0:T(8,128)}) custom-call(s32[1]{0:T(128)} %dynamic_slice.5.own_scalar, s32[8,128]{1,0:T(8,128)S(1)} %broadcast_in_dim.88.own_cell, f32[1,128]{1,0:T(1,128)S(1)} %broadcast_in_dim.89.keep_ref, f32[5,2,8,8,128]{4,3,2,1,0:T(8,128)S(1)} %cut.1.cuts, s32[4,256]{1,0:T(4,128)S(1)} %get-tuple-element.363.signs_ref, ...), custom_call_target="tpu_custom_call" | custom-call | tf_op jit(solution)/shard_map/while/body/sketch/pallas_call | solution.py:495
  65.6 4.3 %finish.1 = (f32[64,4096]{1,0:T(8,128)}, f32[64,64]{1,0:T(8,128)}) custom-call(f32[2,16,128]{2,1,0:T(8,128)} %get-tuple-element.178.gram_ref, f32[64,4096]{1,0:T(8,128)S(1)} %get-tuple-element.179.sketch_ref), custom_call_target="tpu_custom_call" | custom-call | tf_op jit(solution)/shard_map/finish/pallas_call | solution.py:549
  (4 shorter events, 0.0 us)
Async XLA Ops:
  0.7 0.7 copy-start.3
  5.4 0.9 %copy-start = (f32[8,8192]{1,0:T(8,128)S(1)}, f32[8,8192]{1,0:T(8,128)}, u32[]{:S(2)}) copy-start(f32[8,8192]{1,0:T(8,128)} %param.6) | copy-start | bytes 786436
  5.4 1.0 %copy-start.1 = (f32[8,8192]{1,0:T(8,128)S(1)}, f32[8,8192]{1,0:T(8,128)}, u32[]{:S(2)}) copy-start(f32[8,8192]{1,0:T(8,128)} %param.7) | copy-start | bytes 786436
  5.4 1.0 %copy-start.2 = (s32[4,256]{1,0:T(4,128)S(1)}, s32[4,256]{1,0:T(4,128)}, u32[]{:S(2)}) copy-start(s32[4,256]{1,0:T(4,128)} %param.8) | copy-start | bytes 12292

commit v3 on v2

--- a/solution.py
+++ b/solution.py
@@ -80,22 +80,43 @@
     )
 
 
-def cut_kernel(cells_ref, cond_ref, leak_ref, out_ref):
-    me = lax.axis_index("probe")
-    lane = lanes()
-    for e in range(SPAN):
-        _, _, y_first, _, z_first = decode(cells_ref[me % 2 * (SLOTS // 2) + me // 2 * SPAN + e])
-        pair_first = y_first // 2
-        shifts = [wrap(128 - z_first), wrap(96 - z_first), wrap(192 - z_first), wrap(160 - z_first)]
-        for k in range(QUADS):
-            one = pl.multiple_of(jnp.clip(pair_first + 2 * k, 0, 63) * 128, 128)
-            two = pl.multiple_of(jnp.clip(pair_first + 2 * k + 1, 0, 63) * 128, 128)
-            for prop, ref in enumerate((cond_ref, leak_ref)):
-                a = ref[:, pl.ds(one, 128)]
-                b = ref[:, pl.ds(two, 128)]
-                low = jnp.where(lane < 32, pltpu.roll(a, shifts[0], 1), pltpu.roll(a, shifts[1], 1))
-                high = jnp.where(lane < 96, pltpu.roll(b, shifts[2], 1), pltpu.roll(b, shifts[3], 1))
-                out_ref[e, prop, k] = jnp.where(lane < 64, low, high)
+def quads(block):
+    return range(QUADS) if 0 < block < SPAN - 1 else range(2, 6)
+
+
+def counted(owner, first, rows):
+    shape = (rows, 256)
+    lane = lanes(shape)
+    ones = jnp.where(jnp.broadcast_to(owner, shape) == sublanes(shape) + first, 1, 0)
+    total = ones
+    for step in (1, 2, 4, 8, 16, 32, 64, 128):
+        total = total + jnp.where(lane >= step, pltpu.roll(total, step, 1), 0)
+    return ones, total - ones
+
+
+def cut(cell, cell_row, e, cond_ref, leak_ref, out_ref):
+    pair_first = lax.shift_right_arithmetic(decode(cell)[2], 1)
+    shape = (256, 128)
+    z_first = decode(jnp.broadcast_to(cell_row, shape))[4]
+    row = sublanes(shape)
+    lane = lanes(shape)
+    same = lax.shift_right_logical(row, 6) == lax.shift_right_logical(lane, 5)
+    hit = same & (lax.bitwise_and(row, 63) - z_first == lax.bitwise_and(lane, 31))
+    move = jnp.where(hit, 1.0, 0.0).astype(jnp.bfloat16)
+    parts = []
+    for ref in (cond_ref, leak_ref):
+        for k in quads(e):
+            one = ref[jnp.clip(pair_first + 2 * k, 0, 63)]
+            two = ref[jnp.clip(pair_first + 2 * k + 1, 0, 63)]
+            parts.append(jnp.concatenate([one, two], axis=1))
+    rows = 8 * len(parts)
+    both = jnp.concatenate(split2(jnp.concatenate(parts, axis=0)), axis=0)
+    both = jnp.dot(both, move, preferred_element_type=F32)
+    both = both[:rows] + both[rows:]
+    for n, k in enumerate(quads(e)):
+        for prop in range(2):
+            at = 8 * (n + prop * len(quads(e)))
+            out_ref[e, prop, k] = both[at : at + 8]
 
 
 def faces(cell, here, win_ref, coef):
@@ -108,7 +129,7 @@
     for b in range(SPAN):
         xx = (here + (b - REACH)) * 8 + sub
         x_ok = (xx >= 0) & (xx < 256)
-        for k in range(QUADS):
+        for k in quads(b):
             yy = y_first + 4 * k + group
             inside = x_ok & (yy >= 0) & (yy < 128) & z_ok
             own = win_ref[b, 0, k]
@@ -164,7 +185,7 @@
         k_low, k_high = (15 - wide) // 4, (16 + wide) // 4
         b_low, b_high = (1, 3) if wide <= 8 else (0, 4)
         for b in range(b_low, b_high + 1):
-            for k in range(k_low, k_high + 1):
+            for k in range(max(k_low, quads(b)[0]), min(k_high, quads(b)[-1]) + 1):
                 own = search[now, b, k]
                 edge = pltpu.roll(search[now, b - 1, k], 1, 0) if b > 0 else zero
                 down = jnp.where(sub == 0, edge, pltpu.roll(own, 1, 0))
@@ -214,14 +235,23 @@
         out_ref[b, :, k, :] = both[8 * k : 8 * k + 8]
 
 
-def panel(signs, slot_ref, cell_lane, cell_down, half, keep, before_ref, rows_ref, out_ref):
-    table = jnp.concatenate([signs[p % 2, p // 2] for p in range(GROUP)], axis=0)
-    table = (2 * table - 1).astype(jnp.bfloat16)
-    which = lax.broadcasted_iota(jnp.int32, (256, 128), 0) == slot_ref[...]
-    pick = jnp.dot(table, which.astype(F32).astype(jnp.bfloat16), preferred_element_type=F32)
-    _, _, y_first, _, _ = decode(cell_lane[...])
-    pair_first = lax.shift_right_arithmetic(y_first, 1) - PAIRS * half
-    _, _, _, _, z_first = decode(cell_down[...])
+def slots(ones, counts, wells, turn, chip):
+    shape = (GROUP, 256)
+    place = sublanes(shape)
+    probe = 2 * lax.bitwise_and(chip - lax.bitwise_and(place, 7), 7) + lax.shift_right_logical(place, 3)
+    want = probe + GROUP * jnp.broadcast_to(turn, shape)
+    parts = []
+    for e in range(SPAN):
+        there = jnp.broadcast_to(ones[e : e + 1], shape) > 0
+        parts.append(there & (jnp.broadcast_to(counts[e : e + 1], shape) == want))
+    holds = [jnp.where(part, 1.0, 0.0) for part in parts]
+    wells = jnp.broadcast_to(wells, shape)
+    cells = [jnp.max(jnp.where(part, wells, -1), axis=1, keepdims=True) for part in parts]
+    return jnp.concatenate(holds, axis=0), jnp.concatenate(cells, axis=0)
+
+
+def panel(pick, pair_first, z_first, half, keep, before_ref, rows_ref, out_ref):
+    pair_first = pair_first - float(PAIRS) * half.astype(F32)
     lane = lanes((SLOTS, 128))
     z_here = lane % 64 - z_first
     shown = (z_here >= 0) & (z_here < 32)
@@ -256,17 +286,21 @@
 
 
 def sketch_kernel(
-    own_scalar,
-    own_cell,
-    keep_ref,
-    cuts,
-    signs_ref,
-    slot_ref,
-    cell_lane,
-    cell_down,
+    turn_ref,
+    wells_hbm,
+    cond_hbm,
+    leak_hbm,
+    signs_hbm,
     before_ref,
     sketch_ref,
     gram_ref,
+    rounds_ref,
+    wells_ref,
+    cond_ref,
+    leak_ref,
+    cond_pairs,
+    leak_pairs,
+    cuts,
     win,
     signs,
     coef,
@@ -274,19 +308,22 @@
     resid,
     total,
     fields,
-    block,
     rows,
     move,
+    pick_ref,
+    first_ref,
+    depth_ref,
     mine,
     twin_buf,
     y_buf,
     z_buf,
     x_buf,
+    load_sem,
     win_sem,
     sign_sem,
     sign_pair,
-    near_sem,
-    row_sem,
+    row_send,
+    row_recv,
     pair_sem,
     twin_sem,
     y_sem,
@@ -307,73 +344,106 @@
     ring_x = [(lax.rem(x + r, 4) * 8 + z, me) for r in range(1, 4)]
     twin = (here, chip * 2 + 1 - core)
     entered = barrier_with(near + along + [twin] + ring_z + ring_x)
-    cell = own_cell[...]
-    start_fields(cell, here, search, resid, total)
-    move[...] = moves(cell)
+    loads = []
+    pieces = ((wells_hbm, wells_ref), (cond_hbm, cond_ref), (leak_hbm, leak_ref), (signs_hbm, signs.at[core, chip]))
+    for i, (src, dst) in enumerate(pieces):
+        loads.append(pltpu.make_async_copy(src, dst, load_sem.at[i]))
+        loads[-1].start()
+    one = jnp.ones((8, 128), F32)
+    for b in (0, SPAN - 1):
+        for k in range(QUADS):
+            if k not in quads(b):
+                win[b, 0, k] = one
+    loads[0].wait()
+    wells = wells_ref[...]
+    turn = turn_ref[...]
+    owner = lax.shift_right_logical(wells, 16)
+    ones, counts = counted(owner, here - REACH, 8)
+    chosen = (ones > 0) & (counts == me + GROUP * jnp.broadcast_to(turn, (8, 256)))
+    cells = jnp.max(jnp.where(chosen, jnp.broadcast_to(wells, (8, 256)), -1), axis=1, keepdims=True)
+    cell = jnp.broadcast_to(cells[REACH : REACH + 1], (8, 128))
+    for copy in loads[1:]:
+        copy.wait()
+    for src, dst in ((cond_ref, cond_pairs), (leak_ref, leak_pairs)):
+        for t in range(64):
+            dst[t] = src[:, 128 * t : 128 * t + 128]
+    for e in range(SPAN):
+        cut(cells[e, 0], cells[e : e + 1], e, cond_pairs, leak_pairs, cuts)
     entered()
     sent = []
     windows = []
     for i, d in enumerate(OFFSETS):
-        copy = remote(cuts.at[d + 2], win.at[2 - d], win_sem.at[0, i], win_sem.at[1, i], near[i])
+        src, dst = cuts.at[d + 2], win.at[2 - d]
+        if d in (-2, 2):
+            src, dst = cuts.at[d + 2, :, pl.ds(2, 4)], win.at[2 - d, :, pl.ds(2, 4)]
+        copy = remote(src, dst, win_sem.at[0, i], win_sem.at[1, i], near[i])
         copy.start()
         windows.append(copy)
     shared = []
     for r in range(1, CHIPS):
-        copy = remote(signs_ref, signs.at[core, chip], sign_sem.at[0, r], sign_sem.at[1, r], along[r - 1])
+        part = signs.at[core, chip]
+        copy = remote(part, part, sign_sem.at[0, r], sign_sem.at[1, r], along[r - 1])
         copy.start()
         shared.append(copy)
     win[REACH] = cuts[REACH]
-    signs[core, chip] = signs_ref[...]
+    start_fields(cell, here, search, resid, total)
+    move[...] = moves(cell)
+    all_ones, all_counts = counted(owner, 0, count)
+    rounds_ref[0] = lax.shift_right_logical(jnp.max(jnp.where(all_ones > 0, all_counts, 0)), 4) + 1
+    holds, slot_cells = slots(ones, counts, wells, turn, chip)
+    _, _, y_first, _, z_first = decode(jnp.broadcast_to(slot_cells, (SLOTS, 128)))
+    depth_ref[...] = z_first
+    pairs_first = lax.shift_right_arithmetic(y_first, 1).astype(F32)
+    pairs_first = jnp.concatenate([pairs_first, jnp.zeros((128 - SLOTS, 128), F32)], axis=0)
+    first_ref[...] = pairs_first.T
     for copy in windows:
         copy.wait_recv()
     faces(cell, here, win, coef)
     sweeps(coef, search, resid, total)
-    spread = []
     last = (SWEEPS - 1) % 2
     for b in range(SPAN):
         for k in range(QUADS):
             total[b, k] = total[b, k] + search[last, b, k]
-    _, _, y_first, _, _ = decode(own_scalar[0])
+    y_first = decode(cells[REACH, 0])[2]
     second = lax.shift_right_arithmetic(y_first, 2)
     first = second + lax.bitwise_and(lax.shift_right_arithmetic(y_first, 1), 1)
-    for i, d in enumerate(OFFSETS):
+    arrivals = {}
+    for d in OFFSETS + (0,):
         align(first, second, d + 2, move, total, fields)
-        copy = remote(
-            fields.at[d + 2], block.at[:, pl.ds(8 * (2 - d), 8)], near_sem.at[0, i], near_sem.at[1, i], near[i]
-        )
-        copy.start()
-        spread.append(copy)
-    align(first, second, REACH, move, total, fields)
-    block[:, 8 * REACH : 8 * REACH + 8] = fields[REACH]
+        e = 2 - d
+        for r in (4, 3, 5, 2, 6, 1, 7, 0):
+            target = lax.rem(chip + r, CHIPS)
+            place = rows.at[pl.ds(pl.multiple_of((e * GROUP + core * CHIPS + r) * 8, 8), 8)]
+            if d == 0 and r == 0:
+                rows[pl.ds(pl.multiple_of((e * GROUP + core * CHIPS) * 8, 8), 8), :] = fields[REACH, chip]
+                continue
+            device = (lax.rem(here + d + count, count), target * 2 + core)
+            copy = remote(fields.at[d + 2, target], place, row_send.at[d + 2, r], row_recv.at[e, r], device)
+            copy.start()
+            arrivals[e, r] = copy
     for copy in shared:
         copy.wait_recv()
     pair = remote(signs.at[core], signs.at[core], sign_pair.at[0], sign_pair.at[1], twin)
     pair.start()
-    sent += windows + shared + spread + [pair]
-    for copy in spread:
-        copy.wait_recv()
-    out = []
-    place = pl.ds(pl.multiple_of((core * CHIPS + chip) * 8 * SPAN, 8), 8 * SPAN)
-    for r in range(1, CHIPS):
-        target = lax.rem(chip + r, CHIPS)
-        copy = remote(block.at[target], rows.at[place], row_sem.at[0, r], row_sem.at[1, r], along[r - 1])
-        copy.start()
-        out.append(copy)
-    rows[place, :] = block[chip]
+    pair.wait_recv()
+    table = jnp.concatenate([signs[p % 2, p // 2] for p in range(GROUP)], axis=0)
+    table = (2 * table - 1).astype(F32).astype(jnp.bfloat16)
+    holds = jnp.concatenate([holds, jnp.zeros((128 - SLOTS, 256), F32)], axis=0).astype(jnp.bfloat16)
+    pick_ref[...] = lax.dot_general(table, holds, (((1,), (1,)), ((), ())), preferred_element_type=F32)
     pairs = []
-    for r in (0, 1, 7, 2, 6, 3, 5, 4):
-        source = lax.rem(chip - r + CHIPS, CHIPS)
-        if r:
-            out[r - 1].wait_recv()
-        part = rows.at[pl.ds(pl.multiple_of((core * CHIPS + source) * 8 * SPAN, 8), 8 * SPAN)]
-        copy = remote(part, part, pair_sem.at[0, r], pair_sem.at[1, r], twin)
+    for e in (2, 1, 3, 0, 4):
+        for r in range(CHIPS):
+            if (e, r) != (REACH, 0):
+                arrivals[e, r].wait_recv()
+        part = rows.at[pl.ds(pl.multiple_of((e * GROUP + core * CHIPS) * 8, 8), 8 * CHIPS)]
+        copy = remote(part, part, pair_sem.at[0, e], pair_sem.at[1, e], twin)
         copy.start()
         pairs.append(copy)
-    pair.wait_recv()
     for copy in pairs:
         copy.wait_recv()
-    sent += out + pairs
-    panel(signs, slot_ref, cell_lane, cell_down, core, keep_ref[...], before_ref, rows, sketch_ref)
+    sent += windows + shared + [pair] + list(arrivals.values()) + pairs
+    keep = jnp.where(turn[:, :128] > 0, 1.0, 0.0)
+    panel(pick_ref[...], first_ref[0:1, :], depth_ref[...], core, keep, before_ref, rows, sketch_ref)
     gram = gram_of(sketch_ref)
     for h in range(2):
         mine[h] = jnp.concatenate([gram[32 * h : 32 * h + 16], gram[32 * h + 16 : 32 * h + 32]], axis=1)
@@ -463,65 +533,55 @@
 
 
 def on_device(conductivity, leakage, signs, wells):
-    here = lax.axis_index("space")
-    chip = lax.axis_index("probe") // 2
-    core = lax.axis_index("probe") % 2
     cells = conductivity.shape[0] * conductivity.shape[1]
     probes = signs.shape[0] * GROUP
     count = wells.shape[0]
-    owner = wells // cells
-    index = jnp.arange(count, dtype=jnp.int32)
-    rank = jnp.sum((owner[None, :] == owner[:, None]) & (index[None, :] < index[:, None]), axis=1, dtype=jnp.int32)
-    rounds = jnp.max(rank) // GROUP + 1
-    slot = jnp.arange(128, dtype=jnp.int32)
-    slot_probe = jnp.where(slot < SLOTS, (slot % (SLOTS // 2)) // SPAN * 2 + slot // (SLOTS // 2), count)
-    slot_block = here + slot % SPAN - REACH
+    wells = wells.reshape(1, count)
 
     def body(carry):
-        turn, sketch, _ = carry
-        match = (owner[None, :] == slot_block[:, None]) & (rank[None, :] - turn * GROUP == slot_probe[:, None])
-        chosen = jnp.max(jnp.where(match, index[None, :], -1), axis=1)
-        cell = jnp.max(jnp.where(match, wells[None, :], -1), axis=1)
-        cuts = pl.pallas_call(
-            cut_kernel,
-            out_shape=jax.ShapeDtypeStruct((SPAN, 2, QUADS, 8, 128), F32),
-            in_specs=[whole(SMEM), whole(), whole()],
-            out_specs=whole(),
-            compiler_params=params(),
-            name="cut",
-        )(cell, conductivity, leakage)
-        own = cell[core * (SLOTS // 2) + chip * SPAN + REACH]
+        turn, _, sketch, _ = carry
         field = VMEM((SPAN, QUADS, 8, 128), F32)
-        sketch, gram = pl.pallas_call(
+        window = VMEM((SPAN, 2, QUADS, 8, 128), F32)
+        sketch, gram, rounds = pl.pallas_call(
             sketch_kernel,
             out_shape=(
                 jax.ShapeDtypeStruct(sketch.shape, F32),
                 jax.ShapeDtypeStruct((2, 16, 128), F32),
+                jax.ShapeDtypeStruct((1,), jnp.int32),
             ),
-            in_specs=[whole(SMEM)] + [whole()] * 8,
-            out_specs=(whole(), whole()),
+            in_specs=[whole()] + [whole(pltpu.HBM)] * 4 + [whole()],
+            out_specs=(whole(), whole(), whole(SMEM)),
             scratch_shapes=[
-                VMEM((SPAN, 2, QUADS, 8, 128), F32),
+                VMEM((1, count), jnp.int32),
+                VMEM(conductivity.shape, F32),
+                VMEM(leakage.shape, F32),
+                VMEM((64, 8, 128), F32),
+                VMEM((64, 8, 128), F32),
+                window,
+                window,
                 VMEM((2, CHIPS, probes // GROUP, count), jnp.int32),
                 VMEM((7, SPAN, QUADS, 8, 128), F32),
                 VMEM((2, SPAN, QUADS, 8, 128), F32),
                 field,
                 field,
                 VMEM((SPAN, 8, QUADS, 128), F32),
-                VMEM((8, SPAN * QUADS, 128), F32),
                 VMEM((SLOTS * QUADS, 128), F32),
                 VMEM((256, 128), jnp.bfloat16),
+                VMEM((probes, 128), F32),
+                VMEM((128, 128), F32),
+                VMEM((SLOTS, 128), jnp.int32),
                 VMEM((2, 16, 128), F32),
                 VMEM((16, 128), F32),
                 VMEM((8, 16, 128), F32),
                 VMEM((8, 16, 128), F32),
                 VMEM((4, 16, 128), F32),
+                dma(4),
                 dma(2, 4),
                 dma(2, 8),
                 dma(2),
-                dma(2, 4),
-                dma(2, 8),
-                dma(2, 8),
+                dma(SPAN, 8),
+                dma(SPAN, 8),
+                dma(2, SPAN),
                 dma(2),
                 dma(2, 8),
                 dma(2, 8),
@@ -530,22 +590,13 @@
             ],
             compiler_params=params(collective_id=0, has_side_effects=True),
             name="sketch",
-        )(
-            own.reshape(1),
-            jnp.broadcast_to(own, (8, 128)),
-            jnp.broadcast_to((turn > 0).astype(F32), (1, 128)),
-            cuts,
-            signs,
-            chosen[None, :],
-            cell[None, :],
-            jnp.broadcast_to(cell[:SLOTS, None], (SLOTS, 128)),
-            sketch,
-        )
-        return turn + 1, sketch, gram
+        )(jnp.broadcast_to(turn, (1, count)), wells, conductivity, leakage, signs, sketch)
+        return turn + 1, rounds[0], sketch, gram
 
     sketch = jnp.zeros((probes, cells // GROUP), F32)
     gram = jnp.zeros((2, 16, 128), F32)
-    _, sketch, gram = lax.while_loop(lambda carry: carry[0] < rounds, body, (jnp.int32(0), sketch, gram))
+    start = (jnp.int32(0), jnp.int32(1), sketch, gram)
+    _, _, sketch, gram = lax.while_loop(lambda carry: carry[0] < carry[1], body, start)
     return pl.pallas_call(
         finish_kernel,
         out_shape=(

time: 70.1 us -> 58.6 us (0.84)
  Pallas kernels: 61.7 us -> 55.3 us
  between operations: 3.29 us -> 0.65 us
  local copies, waits for them, and re-layouts: 3.72 us -> 1.69 us
  other arithmetic: 1.05 us -> 0 us
    pallas_call x1, Pallas kernels: 56.5 us -> 51.1 us  [body(): pl.pallas_call(sketch_kernel, out_shape=(jax.ShapeDtypeStruct(sketch.shap...]
    pallas_call x1 -> x0, Pallas kernels: 0.98 us -> none  [body(): pl.pallas_call(cut_kernel, out_shape=jax.ShapeDtypeStruct((SPAN, 2, QUADS...]
    reduce_max x2 -> x0, other arithmetic: 0.83 us -> none  [the longest x1 0.64 us: on_device(): rounds = jnp.max(rank) // GROUP + 1]
    broadcast_in_dim x3 -> x1, local copies, waits for them, and re-layouts: 0.71 us -> 0.01 us  [body(): jnp.broadcast_to(turn, (1, count))]
where the time goes in v3:
time: 58.6 us; the launch traced here: 58.4 us
  Pallas kernels  55.3 us (94%)
  local copies, waits for them, and re-layouts  1.69 us (3%)
  loops' own time  0.71 us (1%)
  between operations  0.65 us (1%)
    pallas_call x1, Pallas kernels, body(): pl.pallas_call(sketch_kernel, out_shape=(jax.ShapeDtypeStruct(sketch.shap...  51.1 us
    pallas_call x1, Pallas kernels, on_device(): pl.pallas_call(finish_kernel, out_shape=(jax.ShapeDtypeStruct((probes, ce...  4.27 us

profile of v3, /device:TPU:1, one launch (start us, length us, event | category | flops | bytes accessed | tf_op | source)
XLA Modules:
  0.0 58.4 jit_solution(17788779048468884049)
XLA Ops:
  0.6 0.6 %broadcast_in_dim.10 = f32[2,16,128]{2,1,0:T(8,128)} broadcast(f32[]{:T(128)} %constant.2.clone.1), dimensions={} | broadcast | bytes 16388 | tf_op jit(solution)/shard_map/broadcast_in_dim | solution.py:597
  1.2 0.0 copy-start
  1.2 0.0 copy-start.1
  1.2 0.0 copy-start.2
  1.2 0.0 copy-start.3
  1.2 0.1 broadcast_in_dim.9
  1.3 0.9 %copy-done = f32[8,8192]{1,0:T(8,128)S(1)} copy-done((f32[8,8192]{1,0:T(8,128)S(1)}, f32[8,8192]{1,0:T(8,128)}, u32[]{:S(2)}) %copy-start) | copy-done | bytes 262168
  2.2 0.1 copy-done.1
  2.3 0.0 copy-done.2
  2.3 0.0 copy-done.3
  2.3 51.8 %while.14 = (s32[]{:T(128)}, s32[]{:T(128)}, f32[64,4096]{1,0:T(8,128)S(1)}, f32[2,16,128]{2,1,0:T(8,128)}, s32[1,256]{1,0:T(1,128)S(1)}, /*index=5*/f32[8,8192]...) while((s32[]{:T(128)}, s32[]{:T(128)}, f32[64,4096]{1,0:T(8,128)S(1)}, ...), condition=%wide.region_1.0_spmd, body=%wide.region_0.0_spmd.sunk | while | flops 2 | bytes 2098281 | solution.py:599
  2.3 0.1 copy.21.before_ref
  2.3 51.1 %sketch.1 = (f32[64,4096]{1,0:T(8,128)S(1)}, f32[2,16,128]{2,1,0:T(8,128)}, s32[1]{0:T(128)}) custom-call(s32[1,256]{1,0:T(1,128)S(1)} %broadcast_in_dim.12.turn_ref, s32[1,256]{1,0:T(1,128)S(1)} %get-tuple-element.139.wells_hbm, f32[8,8192]{1,0:T(8,128)S(1)} %get-tuple-element.140.cond_hbm, f32[8,8192]{1,0:T(8,128)S(1)} %get-tuple-element.141.leak_hbm, ...), custom_call_target="tpu_custom_call" | custom-call | tf_op jit(solution)/shard_map/while/body/sketch/pallas_call | solution.py:545
  54.1 4.3 %finish.1 = (f32[64,4096]{1,0:T(8,128)}, f32[64,64]{1,0:T(8,128)}) custom-call(f32[2,16,128]{2,1,0:T(8,128)} %get-tuple-element.47.gram_ref, f32[64,4096]{1,0:T(8,128)S(1)} %get-tuple-element.48.sketch_ref), custom_call_target="tpu_custom_call" | custom-call | tf_op jit(solution)/shard_map/finish/pallas_call | solution.py:600
  (1 shorter events, 0.0 us)
Async XLA Ops:
  1.2 0.9 %copy-start = (f32[8,8192]{1,0:T(8,128)S(1)}, f32[8,8192]{1,0:T(8,128)}, u32[]{:S(2)}) copy-start(f32[8,8192]{1,0:T(8,128)} %param.6) | copy-start | bytes 786436
  1.2 1.0 %copy-start.1 = (f32[8,8192]{1,0:T(8,128)S(1)}, f32[8,8192]{1,0:T(8,128)}, u32[]{:S(2)}) copy-start(f32[8,8192]{1,0:T(8,128)} %param.7) | copy-start | bytes 786436
  1.2 1.0 %copy-start.2 = (s32[4,256]{1,0:T(4,128)S(1)}, s32[4,256]{1,0:T(4,128)}, u32[]{:S(2)}) copy-start(s32[4,256]{1,0:T(4,128)} %param.8) | copy-start | bytes 12292
  1.2 1.0 %copy-start.3 = (s32[256]{0:T(256)S(1)}, s32[256]{0:T(256)}, u32[]{:S(2)}) copy-start(s32[256]{0:T(256)} %param.9) | copy-start | bytes 3076

commit v4 on v3

--- a/solution.py
+++ b/solution.py
@@ -15,6 +15,9 @@
 GROUP = 16
 CHIPS = 8
 SLOTS = GROUP * SPAN
+ORDER = (2, 1, 3, 0, 4)
+EARLY = 3 * GROUP
+LATE = SLOTS - EARLY
 QUADS = 8
 PAIRS = 32
 
@@ -119,22 +122,22 @@
             out_ref[e, prop, k] = both[at : at + 8]
 
 
-def faces(cell, here, win_ref, coef):
+def faces(cell, here, blocks, low, high, win_ref, coef):
     _, _, y_first, _, z_first = decode(cell)
     lane = lanes()
     sub = sublanes()
     group = lane // 32
     zz = z_first + lane % 32
     z_ok = (zz >= 0) & (zz < NZ)
-    for b in range(SPAN):
+    for b in blocks:
         xx = (here + (b - REACH)) * 8 + sub
         x_ok = (xx >= 0) & (xx < 256)
         for k in quads(b):
             yy = y_first + 4 * k + group
             inside = x_ok & (yy >= 0) & (yy < 128) & z_ok
             own = win_ref[b, 0, k]
-            before = win_ref[max(b - 1, 0), 0, k]
-            after = win_ref[min(b + 1, SPAN - 1), 0, k]
+            before = win_ref[max(b - 1, low), 0, k]
+            after = win_ref[min(b + 1, high), 0, k]
             left = win_ref[b, 0, max(k - 1, 0)]
             right = win_ref[b, 0, min(k + 1, QUADS - 1)]
             parts = (
@@ -173,12 +176,12 @@
             total[b, k] = zero
 
 
-def sweeps(coef, search, resid, total):
+def sweeps(steps, coef, search, resid, total):
     group = lanes() // 32
     sub = sublanes()
     zero = jnp.zeros((8, 128), F32)
     table = chebyshev_table(SWEEPS)
-    for j in range(SWEEPS - 1):
+    for j in steps:
         a, c = (float(value) for value in table[j])
         now, later = j % 2, (j + 1) % 2
         wide = j + 1
@@ -241,7 +244,7 @@
     probe = 2 * lax.bitwise_and(chip - lax.bitwise_and(place, 7), 7) + lax.shift_right_logical(place, 3)
     want = probe + GROUP * jnp.broadcast_to(turn, shape)
     parts = []
-    for e in range(SPAN):
+    for e in ORDER:
         there = jnp.broadcast_to(ones[e : e + 1], shape) > 0
         parts.append(there & (jnp.broadcast_to(counts[e : e + 1], shape) == want))
     holds = [jnp.where(part, 1.0, 0.0) for part in parts]
@@ -250,15 +253,15 @@
     return jnp.concatenate(holds, axis=0), jnp.concatenate(cells, axis=0)
 
 
-def panel(pick, pair_first, z_first, half, keep, before_ref, rows_ref, out_ref):
+def panel(pick, pair_first, z_first, half, first, number, rows_ref, add):
     pair_first = pair_first - float(PAIRS) * half.astype(F32)
-    lane = lanes((SLOTS, 128))
-    z_here = lane % 64 - z_first
+    lane = lanes((number, 128))
+    z_here = lane % 64 - z_first[first : first + number]
     shown = (z_here >= 0) & (z_here < 32)
     group = lane // 32
-    blank = jnp.zeros((128 - SLOTS, 128), jnp.bfloat16)
+    rest = 64 - number
     for k in range(QUADS):
-        own = rows_ref[pl.ds(k, SLOTS, stride=8), :]
+        own = rows_ref[pl.ds(first * 8 + k, number, stride=8), :]
         r1, r2, r3 = (pltpu.roll(own, 32 * n, 1) for n in (1, 2, 3))
         pairs = (
             jnp.where(group == 0, own, jnp.where(group == 3, r2, r1)),
@@ -266,21 +269,25 @@
         )
         for m in range(2):
             high, low = split2(jnp.where(shown, pairs[m], 0.0))
+            blank = jnp.zeros((rest, 128), jnp.bfloat16)
             value = jnp.concatenate([high, blank, low, blank], axis=0)
             left = []
             for t in (2 * k + m, 2 * k + m + 16):
                 ok = (pair_first <= t) & (t < pair_first + 16)
                 left.append(jnp.where(ok, pick, 0.0).astype(jnp.bfloat16))
-            left = jnp.concatenate(left, axis=0)
-            both = jnp.dot(jnp.concatenate([left, left], axis=1), value, preferred_element_type=F32)
+            both = jnp.dot(jnp.concatenate(left, axis=0), value, preferred_element_type=F32)
             for n in range(2):
-                at = 128 * (2 * k + m + 16 * n)
-                part = both[64 * n : 64 * n + 64]
-                out_ref[:, at : at + 128] = part + keep * before_ref[:, at : at + 128]
+                add(128 * (2 * k + m + 16 * n), both[64 * n : 64 * n + 64])
+
+
+def doubled(value, first, number):
+    lane = lanes(value.shape)
+    low = pltpu.roll(value, (128 - first) % 128, 1) if first else value
+    return jnp.where(lane % 64 < number, jnp.where(lane < 64, low, pltpu.roll(value, (192 - first) % 128, 1)), 0.0)
 
 
 def gram_of(sketch_ref):
-    both = jnp.concatenate(split2(sketch_ref[...]), axis=0)
+    both = jnp.concatenate(split2(sketch_ref[:64, :]), axis=0)
     full = lax.dot_general(both, both, (((1,), (1,)), ((), ())), preferred_element_type=F32)
     return full[:64, :64] + ((full[:64, 64:] + full[64:, :64]) + full[64:, 64:])
 
@@ -293,7 +300,6 @@
     signs_hbm,
     before_ref,
     sketch_ref,
-    gram_ref,
     rounds_ref,
     wells_ref,
     cond_ref,
@@ -313,6 +319,7 @@
     pick_ref,
     first_ref,
     depth_ref,
+    gram_ref,
     mine,
     twin_buf,
     y_buf,
@@ -395,11 +402,15 @@
     depth_ref[...] = z_first
     pairs_first = lax.shift_right_arithmetic(y_first, 1).astype(F32)
     pairs_first = jnp.concatenate([pairs_first, jnp.zeros((128 - SLOTS, 128), F32)], axis=0)
-    first_ref[...] = pairs_first.T
-    for copy in windows:
+    pairs_first = pairs_first.T
+    for copy in windows[2:]:
         copy.wait_recv()
-    faces(cell, here, win, coef)
-    sweeps(coef, search, resid, total)
+    faces(cell, here, (1, 2, 3), 1, 3, win, coef)
+    sweeps(range(8), coef, search, resid, total)
+    for copy in windows[:2]:
+        copy.wait_recv()
+    faces(cell, here, (0, 1, 3, 4), 0, 4, win, coef)
+    sweeps(range(8, SWEEPS - 1), coef, search, resid, total)
     last = (SWEEPS - 1) % 2
     for b in range(SPAN):
         for k in range(QUADS):
@@ -413,9 +424,9 @@
         e = 2 - d
         for r in (4, 3, 5, 2, 6, 1, 7, 0):
             target = lax.rem(chip + r, CHIPS)
-            place = rows.at[pl.ds(pl.multiple_of((e * GROUP + core * CHIPS + r) * 8, 8), 8)]
+            place = rows.at[pl.ds(pl.multiple_of((ORDER.index(e) * GROUP + core * CHIPS + r) * 8, 8), 8)]
             if d == 0 and r == 0:
-                rows[pl.ds(pl.multiple_of((e * GROUP + core * CHIPS) * 8, 8), 8), :] = fields[REACH, chip]
+                rows[pl.ds(pl.multiple_of((ORDER.index(e) * GROUP + core * CHIPS) * 8, 8), 8), :] = fields[REACH, chip]
                 continue
             device = (lax.rem(here + d + count, count), target * 2 + core)
             copy = remote(fields.at[d + 2, target], place, row_send.at[d + 2, r], row_recv.at[e, r], device)
@@ -429,21 +440,36 @@
     table = jnp.concatenate([signs[p % 2, p // 2] for p in range(GROUP)], axis=0)
     table = (2 * table - 1).astype(F32).astype(jnp.bfloat16)
     holds = jnp.concatenate([holds, jnp.zeros((128 - SLOTS, 256), F32)], axis=0).astype(jnp.bfloat16)
-    pick_ref[...] = lax.dot_general(table, holds, (((1,), (1,)), ((), ())), preferred_element_type=F32)
+    pick = lax.dot_general(table, holds, (((1,), (1,)), ((), ())), preferred_element_type=F32)
+    keep = jnp.where(turn[:, :128] > 0, 1.0, 0.0)
+    parts = ((0, EARLY), (EARLY, LATE))
+    for n, (start, number) in enumerate(parts):
+        pick_ref[n] = doubled(pick, start, number)
+        first_ref[n] = doubled(pairs_first[0:8], start, number)
+
+    def put(at, value):
+        sketch_ref[:64, at : at + 128] = value + keep * before_ref[:64, at : at + 128]
+
+    def add(at, value):
+        sketch_ref[:64, at : at + 128] = sketch_ref[:64, at : at + 128] + value
+
     pairs = []
-    for e in (2, 1, 3, 0, 4):
+    for e in ORDER:
         for r in range(CHIPS):
             if (e, r) != (REACH, 0):
                 arrivals[e, r].wait_recv()
-        part = rows.at[pl.ds(pl.multiple_of((e * GROUP + core * CHIPS) * 8, 8), 8 * CHIPS)]
+        part = rows.at[pl.ds(pl.multiple_of((ORDER.index(e) * GROUP + core * CHIPS) * 8, 8), 8 * CHIPS)]
         copy = remote(part, part, pair_sem.at[0, e], pair_sem.at[1, e], twin)
         copy.start()
         pairs.append(copy)
-    for copy in pairs:
+        if e == 3:
+            for copy in pairs:
+                copy.wait_recv()
+            panel(pick_ref[0], first_ref[0, 0:1, :], depth_ref[...], core, 0, EARLY, rows, put)
+    for copy in pairs[3:]:
         copy.wait_recv()
+    panel(pick_ref[1], first_ref[1, 0:1, :], depth_ref[...], core, EARLY, LATE, rows, add)
     sent += windows + shared + [pair] + list(arrivals.values()) + pairs
-    keep = jnp.where(turn[:, :128] > 0, 1.0, 0.0)
-    panel(pick_ref[...], first_ref[0:1, :], depth_ref[...], core, keep, before_ref, rows, sketch_ref)
     gram = gram_of(sketch_ref)
     for h in range(2):
         mine[h] = jnp.concatenate([gram[32 * h : 32 * h + 16], gram[32 * h + 16 : 32 * h + 32]], axis=1)
@@ -469,17 +495,20 @@
     copy = remote(gram_ref.at[core], gram_ref.at[core], last_sem.at[0], last_sem.at[1], twin)
     copy.start()
     copy.wait_recv()
+    for h in range(2):
+        sketch_ref[64:, 128 * h : 128 * h + 128] = gram_ref[h]
     for item in sent + [copy]:
         item.wait_send()
 
 
-def finish_kernel(gram_ref, sketch_ref, basis_ref, factor_ref):
+def finish_kernel(sketch_ref, basis_ref, factor_ref):
     shape = (8, 128)
     lane = lanes(shape)
     sub = sublanes(shape)
     rows = []
     for i in range(8):
-        block = gram_ref[i // 4, 8 * (i % 2) : 8 * (i % 2) + 8, :]
+        at = 128 * (i // 4)
+        block = sketch_ref[64 + 8 * (i % 2) : 72 + 8 * (i % 2), at : at + 128]
         if i % 4 >= 2:
             block = pltpu.roll(block, 64, 1)
         rows.append(jnp.where(lane < 64, block, jnp.where(lane - 64 == sub + 8 * i, 1.0, 0.0)))
@@ -515,7 +544,7 @@
     high, low = split2(full[:, 64:] * math.sqrt(256 * 128 * 64))
     left = jnp.concatenate([high, high, low], axis=1)
     for t in range(8):
-        high, low = split2(sketch_ref[:, 512 * t : 512 * t + 512])
+        high, low = split2(sketch_ref[:64, 512 * t : 512 * t + 512])
         right = jnp.concatenate([high, low, high], axis=0)
         basis_ref[:, 512 * t : 512 * t + 512] = jnp.dot(left, right, preferred_element_type=F32)
 
@@ -539,18 +568,17 @@
     wells = wells.reshape(1, count)
 
     def body(carry):
-        turn, _, sketch, _ = carry
+        turn, _, sketch = carry
         field = VMEM((SPAN, QUADS, 8, 128), F32)
         window = VMEM((SPAN, 2, QUADS, 8, 128), F32)
-        sketch, gram, rounds = pl.pallas_call(
+        sketch, rounds = pl.pallas_call(
             sketch_kernel,
             out_shape=(
                 jax.ShapeDtypeStruct(sketch.shape, F32),
-                jax.ShapeDtypeStruct((2, 16, 128), F32),
                 jax.ShapeDtypeStruct((1,), jnp.int32),
             ),
             in_specs=[whole()] + [whole(pltpu.HBM)] * 4 + [whole()],
-            out_specs=(whole(), whole(), whole(SMEM)),
+            out_specs=(whole(), whole(SMEM)),
             scratch_shapes=[
                 VMEM((1, count), jnp.int32),
                 VMEM(conductivity.shape, F32),
@@ -567,9 +595,10 @@
                 VMEM((SPAN, 8, QUADS, 128), F32),
                 VMEM((SLOTS * QUADS, 128), F32),
                 VMEM((256, 128), jnp.bfloat16),
-                VMEM((probes, 128), F32),
-                VMEM((128, 128), F32),
+                VMEM((2, probes, 128), F32),
+                VMEM((2, 8, 128), F32),
                 VMEM((SLOTS, 128), jnp.int32),
+                VMEM((2, 16, 128), F32),
                 VMEM((2, 16, 128), F32),
                 VMEM((16, 128), F32),
                 VMEM((8, 16, 128), F32),
@@ -591,23 +620,22 @@
             compiler_params=params(collective_id=0, has_side_effects=True),
             name="sketch",
         )(jnp.broadcast_to(turn, (1, count)), wells, conductivity, leakage, signs, sketch)
-        return turn + 1, rounds[0], sketch, gram
-
-    sketch = jnp.zeros((probes, cells // GROUP), F32)
-    gram = jnp.zeros((2, 16, 128), F32)
-    start = (jnp.int32(0), jnp.int32(1), sketch, gram)
-    _, _, sketch, gram = lax.while_loop(lambda carry: carry[0] < carry[1], body, start)
+        return turn + 1, rounds[0], sketch
+
+    sketch = jnp.zeros((probes + 16, cells // GROUP), F32)
+    start = (jnp.int32(0), jnp.int32(1), sketch)
+    _, _, sketch = lax.while_loop(lambda carry: carry[0] < carry[1], body, start)
     return pl.pallas_call(
         finish_kernel,
         out_shape=(
             jax.ShapeDtypeStruct((probes, cells // GROUP), F32),
             jax.ShapeDtypeStruct((probes, probes), F32),
         ),
-        in_specs=[whole(), whole()],
+        in_specs=[whole()],
         out_specs=(whole(), whole()),
         compiler_params=params(),
         name="finish",
-    )(gram, sketch)
+    )(sketch)
 
 
 def solution(mesh):

time: 58.6 us -> 57.6 us (0.983)
    pallas_call x1, Pallas kernels: 4.27 us -> 3.55 us  [on_device(): pl.pallas_call(finish_kernel, out_shape=(jax.ShapeDtypeStruct((probes, ce...]
where the time goes in v4:
time: 57.6 us; the launch traced here: 57.4 us
  Pallas kernels  55.1 us (96%)
  local copies, waits for them, and re-layouts  1.11 us (2%)
  between operations  0.68 us (1%)
  loops' own time  0.58 us (1%)
    pallas_call x1, Pallas kernels, body(): pl.pallas_call(sketch_kernel, out_shape=(jax.ShapeDtypeStruct(sketch.shap...  51.5 us
    pallas_call x1, Pallas kernels, on_device(): pl.pallas_call(finish_kernel, out_shape=(jax.ShapeDtypeStruct((probes, ce...  3.55 us

profile of v4, /device:TPU:1, one launch (start us, length us, event | category | flops | bytes accessed | tf_op | source)
XLA Modules:
  0.0 57.4 jit_solution(8220908120032406461)
XLA Ops:
  0.6 0.0 copy-start.3
  0.6 0.0 copy-start.2
  0.7 0.0 copy-start.1
  0.7 0.0 copy-start
  0.7 0.1 broadcast_in_dim.6
  0.8 0.5 copy-done.3
  1.3 0.0 copy-done.2
  1.3 0.3 copy-done.1
  1.6 0.1 copy-done
  1.7 52.2 %while.12 = (s32[]{:T(128)}, s32[]{:T(128)}, f32[80,4096]{1,0:T(8,128)S(1)}, s32[1,256]{1,0:T(1,128)S(1)}, f32[8,8192]{1,0:T(8,128)S(1)}, /*index=5*/f32[8,8192]{1,0:T(8,128)S(1)}, s32[4,256]{1,0:T(4,128)S(1)}, s32[]{:T(128)}) while((s32[]{:T(128)}, s32[]{:T(128)}, f32[80,4096]{1,0:T(8,128)S(1)}, s32[1,256]{1,0:T(1,128)S(1)}, ...), condition=%wide.region_1.0_spmd, body=%wide.region_0.0_spmd.sunk | while | flops 2 | bytes 2622561 | solution.py:627
  1.7 0.1 copy.18.before_ref
  1.8 51.5 %sketch.1 = (f32[80,4096]{1,0:T(8,128)S(1)}, s32[1]{0:T(128)}) custom-call(s32[1,256]{1,0:T(1,128)S(1)} %broadcast_in_dim.8.turn_ref, s32[1,256]{1,0:T(1,128)S(1)} %get-tuple-element.121.wells_hbm, f32[8,8192]{1,0:T(8,128)S(1)} %get-tuple-element.122.cond_hbm, f32[8,8192]{1,0:T(8,128)S(1)} %get-tuple-element.123.leak_hbm, ...), custom_call_target="tpu_custom_call" | custom-call | tf_op jit(solution)/shard_map/while/body/sketch/pallas_call | solution.py:574
  53.9 3.6 %finish.1 = (f32[64,4096]{1,0:T(8,128)}, f32[64,64]{1,0:T(8,128)}) custom-call(f32[80,4096]{1,0:T(8,128)S(1)} %get-tuple-element.41.sketch_ref), custom_call_target="tpu_custom_call" | custom-call | tf_op jit(solution)/shard_map/finish/pallas_call | solution.py:628
  (1 shorter events, 0.0 us)
Async XLA Ops:
  0.6 0.7 %copy-start.3 = (s32[256]{0:T(256)S(1)}, s32[256]{0:T(256)}, u32[]{:S(2)}) copy-start(s32[256]{0:T(256)} %param.9) | copy-start | bytes 3076
  0.6 0.7 %copy-start.2 = (s32[4,256]{1,0:T(4,128)S(1)}, s32[4,256]{1,0:T(4,128)}, u32[]{:S(2)}) copy-start(s32[4,256]{1,0:T(4,128)} %param.8) | copy-start | bytes 12292
  0.7 1.0 %copy-start.1 = (f32[8,8192]{1,0:T(8,128)S(1)}, f32[8,8192]{1,0:T(8,128)}, u32[]{:S(2)}) copy-start(f32[8,8192]{1,0:T(8,128)} %param.7) | copy-start | bytes 786436
  0.7 1.0 %copy-start = (f32[8,8192]{1,0:T(8,128)S(1)}, f32[8,8192]{1,0:T(8,128)}, u32[]{:S(2)}) copy-start(f32[8,8192]{1,0:T(8,128)} %param.6) | copy-start | bytes 786436

commit v5 on v4

--- a/solution.py
+++ b/solution.py
@@ -319,7 +319,6 @@
     pick_ref,
     first_ref,
     depth_ref,
-    gram_ref,
     mine,
     twin_buf,
     y_buf,
@@ -336,7 +335,6 @@
     y_sem,
     z_sem,
     x_sem,
-    last_sem,
 ):
     count = lax.axis_size("space")
     here = lax.axis_index("space")
@@ -386,12 +384,6 @@
         copy = remote(src, dst, win_sem.at[0, i], win_sem.at[1, i], near[i])
         copy.start()
         windows.append(copy)
-    shared = []
-    for r in range(1, CHIPS):
-        part = signs.at[core, chip]
-        copy = remote(part, part, sign_sem.at[0, r], sign_sem.at[1, r], along[r - 1])
-        copy.start()
-        shared.append(copy)
     win[REACH] = cuts[REACH]
     start_fields(cell, here, search, resid, total)
     move[...] = moves(cell)
@@ -405,6 +397,12 @@
     pairs_first = pairs_first.T
     for copy in windows[2:]:
         copy.wait_recv()
+    shared = []
+    for r in range(1, CHIPS):
+        part = signs.at[core, chip]
+        copy = remote(part, part, sign_sem.at[0, r], sign_sem.at[1, r], along[r - 1])
+        copy.start()
+        shared.append(copy)
     faces(cell, here, (1, 2, 3), 1, 3, win, coef)
     sweeps(range(8), coef, search, resid, total)
     for copy in windows[:2]:
@@ -478,10 +476,10 @@
     sent.append(copy)
     copy.wait_recv()
     value = mine[core] + twin_buf[...]
-    for buf, sem, at, ring in ((y_buf, y_sem, chip, along), (z_buf, z_sem, z, ring_z), (x_buf, x_sem, x, ring_x)):
+    for buf, sem, at, ring in ((y_buf, y_sem, chip, along), (z_buf, z_sem, z, ring_z)):
         buf[at] = value
         steps = []
-        for r, device in enumerate(ring):
+        for r, device in sorted(enumerate(ring), key=lambda item: abs(2 * item[0] + 1 - len(ring))):
             copy = remote(buf.at[at], buf.at[at], sem.at[0, r], sem.at[1, r], device)
             copy.start()
             steps.append(copy)
@@ -489,15 +487,25 @@
             copy.wait_recv()
         sent += steps
         value = buf[0]
-        for r in range(1, len(ring) + 1):
+        for r in range(1, 8):
             value = value + buf[r]
-    gram_ref[core] = value
-    copy = remote(gram_ref.at[core], gram_ref.at[core], last_sem.at[0], last_sem.at[1], twin)
-    copy.start()
-    copy.wait_recv()
+    x_buf[core, x] = value
+    steps = []
+    for r in (2, 1, 3, 0):
+        for other in range(2):
+            if r == 0 and other == 0:
+                continue
+            device = (lax.rem(x + r, 4) * 8 + z, chip * 2 + (1 - core if other else core))
+            part = x_buf.at[core, x]
+            copy = remote(part, part, x_sem.at[0, 4 * other + r], x_sem.at[1, 4 * other + r], device)
+            copy.start()
+            steps.append(copy)
+    for copy in steps:
+        copy.wait_recv()
     for h in range(2):
-        sketch_ref[64:, 128 * h : 128 * h + 128] = gram_ref[h]
-    for item in sent + [copy]:
+        value = ((x_buf[h, 0] + x_buf[h, 1]) + x_buf[h, 2]) + x_buf[h, 3]
+        sketch_ref[64:, 128 * h : 128 * h + 128] = value
+    for item in sent + steps:
         item.wait_send()
 
 
@@ -519,7 +527,6 @@
         for c in range(8):
             pivot = jnp.broadcast_to(columns[c][0][c : c + 1, :], shape)
             scale = lax.rsqrt(pivot)
-            scale = scale * (1.5 - 0.5 * pivot * scale * scale)
             line = jnp.broadcast_to(own[c : c + 1, :], shape) * scale
             columns[c] = [value * scale for value in columns[c]]
             below = jnp.where(sub > c, columns[c][0], 0.0)
@@ -599,11 +606,10 @@
                 VMEM((2, 8, 128), F32),
                 VMEM((SLOTS, 128), jnp.int32),
                 VMEM((2, 16, 128), F32),
-                VMEM((2, 16, 128), F32),
                 VMEM((16, 128), F32),
                 VMEM((8, 16, 128), F32),
                 VMEM((8, 16, 128), F32),
-                VMEM((4, 16, 128), F32),
+                VMEM((2, 4, 16, 128), F32),
                 dma(4),
                 dma(2, 4),
                 dma(2, 8),
@@ -614,8 +620,7 @@
                 dma(2),
                 dma(2, 8),
                 dma(2, 8),
-                dma(2, 4),
-                dma(2),
+                dma(2, 8),
             ],
             compiler_params=params(collective_id=0, has_side_effects=True),
             name="sketch",

time: 57.6 us -> 55.9 us (0.970)
  Pallas kernels: 55.1 us -> 53.4 us
    pallas_call x1, Pallas kernels: 51.5 us -> 50.3 us  [body(): pl.pallas_call(sketch_kernel, out_shape=(jax.ShapeDtypeStruct(sketch.shap...]
where the time goes in v5:
time: 55.9 us; the launch traced here: 55.8 us
  Pallas kernels  53.4 us (96%)
  local copies, waits for them, and re-layouts  1.11 us (2%)
  between operations  0.68 us (1%)
  loops' own time  0.58 us (1%)
    pallas_call x1, Pallas kernels, body(): pl.pallas_call(sketch_kernel, out_shape=(jax.ShapeDtypeStruct(sketch.shap...  50.3 us
    pallas_call x1, Pallas kernels, on_device(): pl.pallas_call(finish_kernel, out_shape=(jax.ShapeDtypeStruct((probes, ce...  3.11 us

profile of v5, /device:TPU:1, one launch (start us, length us, event | category | flops | bytes accessed | tf_op | source)
XLA Modules:
  0.0 55.8 jit_solution(15354602803596975395)
XLA Ops:
  0.6 0.0 copy-start.3
  0.6 0.0 copy-start.2
  0.7 0.0 copy-start.1
  0.7 0.0 copy-start
  0.7 0.1 broadcast_in_dim.6
  0.8 0.5 copy-done.3
  1.3 0.0 copy-done.2
  1.3 0.3 copy-done.1
  1.6 0.1 copy-done
  1.7 51.0 %while.12 = (s32[]{:T(128)}, s32[]{:T(128)}, f32[80,4096]{1,0:T(8,128)S(1)}, s32[1,256]{1,0:T(1,128)S(1)}, f32[8,8192]{1,0:T(8,128)S(1)}, /*index=5*/f32[8,8192]{1,0:T(8,128)S(1)}, s32[4,256]{1,0:T(4,128)S(1)}, s32[]{:T(128)}) while((s32[]{:T(128)}, s32[]{:T(128)}, f32[80,4096]{1,0:T(8,128)S(1)}, s32[1,256]{1,0:T(1,128)S(1)}, ...), condition=%wide.region_1.0_spmd, body=%wide.region_0.0_spmd.sunk | while | flops 2 | bytes 2622561 | solution.py:632
  1.7 0.1 copy.18.before_ref
  1.8 50.3 %sketch.1 = (f32[80,4096]{1,0:T(8,128)S(1)}, s32[1]{0:T(128)}) custom-call(s32[1,256]{1,0:T(1,128)S(1)} %broadcast_in_dim.8.turn_ref, s32[1,256]{1,0:T(1,128)S(1)} %get-tuple-element.121.wells_hbm, f32[8,8192]{1,0:T(8,128)S(1)} %get-tuple-element.122.cond_hbm, f32[8,8192]{1,0:T(8,128)S(1)} %get-tuple-element.123.leak_hbm, ...), custom_call_target="tpu_custom_call" | custom-call | tf_op jit(solution)/shard_map/while/body/sketch/pallas_call | solution.py:581
  52.7 3.1 %finish.1 = (f32[64,4096]{1,0:T(8,128)}, f32[64,64]{1,0:T(8,128)}) custom-call(f32[80,4096]{1,0:T(8,128)S(1)} %get-tuple-element.41.sketch_ref), custom_call_target="tpu_custom_call" | custom-call | tf_op jit(solution)/shard_map/finish/pallas_call | solution.py:633
  (1 shorter events, 0.0 us)
Async XLA Ops:
  0.6 0.7 %copy-start.3 = (s32[256]{0:T(256)S(1)}, s32[256]{0:T(256)}, u32[]{:S(2)}) copy-start(s32[256]{0:T(256)} %param.9) | copy-start | bytes 3076
  0.6 0.7 %copy-start.2 = (s32[4,256]{1,0:T(4,128)S(1)}, s32[4,256]{1,0:T(4,128)}, u32[]{:S(2)}) copy-start(s32[4,256]{1,0:T(4,128)} %param.8) | copy-start | bytes 12292
  0.7 1.0 %copy-start.1 = (f32[8,8192]{1,0:T(8,128)S(1)}, f32[8,8192]{1,0:T(8,128)}, u32[]{:S(2)}) copy-start(f32[8,8192]{1,0:T(8,128)} %param.7) | copy-start | bytes 786436
  0.7 1.0 %copy-start = (f32[8,8192]{1,0:T(8,128)S(1)}, f32[8,8192]{1,0:T(8,128)}, u32[]{:S(2)}) copy-start(f32[8,8192]{1,0:T(8,128)} %param.6) | copy-start | bytes 786436

commit v6 on v5

--- a/solution.py
+++ b/solution.py
@@ -253,15 +253,27 @@
     return jnp.concatenate(holds, axis=0), jnp.concatenate(cells, axis=0)
 
 
-def panel(pick, pair_first, z_first, half, first, number, rows_ref, add):
-    pair_first = pair_first - float(PAIRS) * half.astype(F32)
+def align_far(first, second, b, move, total, out_ref, at):
+    one = split2(jnp.concatenate([total[b, 2 + lax.bitwise_and(k - first - 2, 3)] for k in range(4)], axis=0))
+    two = split2(jnp.concatenate([total[b, 2 + lax.bitwise_and(k - second - 2, 3)] for k in range(4)], axis=0))
+    both = jnp.concatenate([jnp.concatenate(part, axis=1) for part in zip(one, two)], axis=0)
+    both = jnp.dot(both, move[...], preferred_element_type=F32)
+    both = both[:32] + both[32:]
+    for k in range(4):
+        out_ref[at, :, k, :] = both[8 * k : 8 * k + 8]
+
+
+def panel(pick, pair_first, z_first, half, load, quads_here, add):
+    number = z_first.shape[0]
+    width = 2 * quads_here
+    pair_first = pair_first - float(PAIRS) * half.astype(F32) + float(8 - quads_here)
     lane = lanes((number, 128))
-    z_here = lane % 64 - z_first[first : first + number]
+    z_here = lane % 64 - z_first
     shown = (z_here >= 0) & (z_here < 32)
     group = lane // 32
     rest = 64 - number
-    for k in range(QUADS):
-        own = rows_ref[pl.ds(first * 8 + k, number, stride=8), :]
+    for k in range(quads_here):
+        own = load(k)
         r1, r2, r3 = (pltpu.roll(own, 32 * n, 1) for n in (1, 2, 3))
         pairs = (
             jnp.where(group == 0, own, jnp.where(group == 3, r2, r1)),
@@ -271,13 +283,14 @@
             high, low = split2(jnp.where(shown, pairs[m], 0.0))
             blank = jnp.zeros((rest, 128), jnp.bfloat16)
             value = jnp.concatenate([high, blank, low, blank], axis=0)
+            places = range(2 * k + m, PAIRS, width)
             left = []
-            for t in (2 * k + m, 2 * k + m + 16):
-                ok = (pair_first <= t) & (t < pair_first + 16)
+            for t in places:
+                ok = (pair_first <= t) & (t < pair_first + width)
                 left.append(jnp.where(ok, pick, 0.0).astype(jnp.bfloat16))
             both = jnp.dot(jnp.concatenate(left, axis=0), value, preferred_element_type=F32)
-            for n in range(2):
-                add(128 * (2 * k + m + 16 * n), both[64 * n : 64 * n + 64])
+            for n, t in enumerate(places):
+                add(128 * t, both[64 * n : 64 * n + 64])
 
 
 def doubled(value, first, number):
@@ -314,7 +327,9 @@
     resid,
     total,
     fields,
+    far_fields,
     rows,
+    far_rows,
     move,
     pick_ref,
     first_ref,
@@ -418,16 +433,25 @@
     first = second + lax.bitwise_and(lax.shift_right_arithmetic(y_first, 1), 1)
     arrivals = {}
     for d in OFFSETS + (0,):
-        align(first, second, d + 2, move, total, fields)
+        far = d in (-2, 2)
+        if far:
+            align_far(first, second, d + 2, move, total, far_fields, (d + 2) // 4)
+        else:
+            align(first, second, d + 2, move, total, fields)
         e = 2 - d
         for r in (4, 3, 5, 2, 6, 1, 7, 0):
             target = lax.rem(chip + r, CHIPS)
-            place = rows.at[pl.ds(pl.multiple_of((ORDER.index(e) * GROUP + core * CHIPS + r) * 8, 8), 8)]
+            if far:
+                source = far_fields.at[(d + 2) // 4, target]
+                place = far_rows.at[(ORDER.index(e) - 3) * GROUP + core * CHIPS + r]
+            else:
+                source = fields.at[d + 2, target]
+                place = rows.at[pl.ds(pl.multiple_of((ORDER.index(e) * GROUP + core * CHIPS + r) * 8, 8), 8)]
             if d == 0 and r == 0:
                 rows[pl.ds(pl.multiple_of((ORDER.index(e) * GROUP + core * CHIPS) * 8, 8), 8), :] = fields[REACH, chip]
                 continue
             device = (lax.rem(here + d + count, count), target * 2 + core)
-            copy = remote(fields.at[d + 2, target], place, row_send.at[d + 2, r], row_recv.at[e, r], device)
+            copy = remote(source, place, row_send.at[d + 2, r], row_recv.at[e, r], device)
             copy.start()
             arrivals[e, r] = copy
     for copy in shared:
@@ -456,17 +480,28 @@
         for r in range(CHIPS):
             if (e, r) != (REACH, 0):
                 arrivals[e, r].wait_recv()
-        part = rows.at[pl.ds(pl.multiple_of((ORDER.index(e) * GROUP + core * CHIPS) * 8, 8), 8 * CHIPS)]
+        if e in (0, SPAN - 1):
+            part = far_rows.at[pl.ds((ORDER.index(e) - 3) * GROUP + core * CHIPS, CHIPS)]
+        else:
+            part = rows.at[pl.ds(pl.multiple_of((ORDER.index(e) * GROUP + core * CHIPS) * 8, 8), 8 * CHIPS)]
         copy = remote(part, part, pair_sem.at[0, e], pair_sem.at[1, e], twin)
         copy.start()
         pairs.append(copy)
         if e == 3:
             for copy in pairs:
                 copy.wait_recv()
-            panel(pick_ref[0], first_ref[0, 0:1, :], depth_ref[...], core, 0, EARLY, rows, put)
+            panel(
+                pick_ref[0],
+                first_ref[0, 0:1, :],
+                depth_ref[:EARLY, :],
+                core,
+                lambda k: rows[pl.ds(k, EARLY, stride=8), :],
+                QUADS,
+                put,
+            )
     for copy in pairs[3:]:
         copy.wait_recv()
-    panel(pick_ref[1], first_ref[1, 0:1, :], depth_ref[...], core, EARLY, LATE, rows, add)
+    panel(pick_ref[1], first_ref[1, 0:1, :], depth_ref[EARLY:, :], core, lambda k: far_rows[:, k, :], 4, add)
     sent += windows + shared + [pair] + list(arrivals.values()) + pairs
     gram = gram_of(sketch_ref)
     for h in range(2):
@@ -600,7 +635,9 @@
                 field,
                 field,
                 VMEM((SPAN, 8, QUADS, 128), F32),
-                VMEM((SLOTS * QUADS, 128), F32),
+                VMEM((2, 8, 4, 128), F32),
+                VMEM((EARLY * QUADS, 128), F32),
+                VMEM((LATE, 4, 128), F32),
                 VMEM((256, 128), jnp.bfloat16),
                 VMEM((2, probes, 128), F32),
                 VMEM((2, 8, 128), F32),

time: 55.9 us -> 55.7 us (level)
  no operation moved by 1% of the time
where the time goes in v6:
time: 55.7 us; the launch traced here: 55.6 us
  Pallas kernels  53.2 us (96%)
  local copies, waits for them, and re-layouts  1.11 us (2%)
  between operations  0.68 us (1%)
  loops' own time  0.58 us (1%)
    pallas_call x1, Pallas kernels, body(): pl.pallas_call(sketch_kernel, out_shape=(jax.ShapeDtypeStruct(sketch.shap...  50.1 us
    pallas_call x1, Pallas kernels, on_device(): pl.pallas_call(finish_kernel, out_shape=(jax.ShapeDtypeStruct((probes, ce...  3.11 us

profile of v6, /device:TPU:1, one launch (start us, length us, event | category | flops | bytes accessed | tf_op | source)
XLA Modules:
  0.0 55.6 jit_solution(17372526253779875002)
XLA Ops:
  0.6 0.0 copy-start.3
  0.6 0.0 copy-start.2
  0.7 0.0 copy-start.1
  0.7 0.0 copy-start
  0.7 0.1 broadcast_in_dim.6
  0.8 0.5 copy-done.3
  1.3 0.0 copy-done.2
  1.3 0.3 copy-done.1
  1.6 0.1 copy-done
  1.7 50.8 %while.12 = (s32[]{:T(128)}, s32[]{:T(128)}, f32[80,4096]{1,0:T(8,128)S(1)}, s32[1,256]{1,0:T(1,128)S(1)}, f32[8,8192]{1,0:T(8,128)S(1)}, /*index=5*/f32[8,8192]{1,0:T(8,128)S(1)}, s32[4,256]{1,0:T(4,128)S(1)}, s32[]{:T(128)}) while((s32[]{:T(128)}, s32[]{:T(128)}, f32[80,4096]{1,0:T(8,128)S(1)}, s32[1,256]{1,0:T(1,128)S(1)}, ...), condition=%wide.region_1.0_spmd, body=%wide.region_0.0_spmd.sunk | while | flops 2 | bytes 2622561 | solution.py:669
  1.7 0.1 copy.18.before_ref
  1.8 50.1 %sketch.1 = (f32[80,4096]{1,0:T(8,128)S(1)}, s32[1]{0:T(128)}) custom-call(s32[1,256]{1,0:T(1,128)S(1)} %broadcast_in_dim.8.turn_ref, s32[1,256]{1,0:T(1,128)S(1)} %get-tuple-element.121.wells_hbm, f32[8,8192]{1,0:T(8,128)S(1)} %get-tuple-element.122.cond_hbm, f32[8,8192]{1,0:T(8,128)S(1)} %get-tuple-element.123.leak_hbm, ...), custom_call_target="tpu_custom_call" | custom-call | tf_op jit(solution)/shard_map/while/body/sketch/pallas_call | solution.py:616
  52.5 3.1 %finish.1 = (f32[64,4096]{1,0:T(8,128)}, f32[64,64]{1,0:T(8,128)}) custom-call(f32[80,4096]{1,0:T(8,128)S(1)} %get-tuple-element.41.sketch_ref), custom_call_target="tpu_custom_call" | custom-call | tf_op jit(solution)/shard_map/finish/pallas_call | solution.py:670
  (1 shorter events, 0.0 us)
Async XLA Ops:
  0.6 0.7 %copy-start.3 = (s32[256]{0:T(256)S(1)}, s32[256]{0:T(256)}, u32[]{:S(2)}) copy-start(s32[256]{0:T(256)} %param.9) | copy-start | bytes 3076
  0.6 0.7 %copy-start.2 = (s32[4,256]{1,0:T(4,128)S(1)}, s32[4,256]{1,0:T(4,128)}, u32[]{:S(2)}) copy-start(s32[4,256]{1,0:T(4,128)} %param.8) | copy-start | bytes 12292
  0.7 1.0 %copy-start.1 = (f32[8,8192]{1,0:T(8,128)S(1)}, f32[8,8192]{1,0:T(8,128)}, u32[]{:S(2)}) copy-start(f32[8,8192]{1,0:T(8,128)} %param.7) | copy-start | bytes 786436
  0.7 1.0 %copy-start = (f32[8,8192]{1,0:T(8,128)S(1)}, f32[8,8192]{1,0:T(8,128)}, u32[]{:S(2)}) copy-start(f32[8,8192]{1,0:T(8,128)} %param.6) | copy-start | bytes 786436
